TPU v7x, 512 devices: a whole 4x4x16 slice. The times are simulated.
512 devices in a mesh: head: 8 (over x, y_hi), seq: 64 (over y_lo, z, core).
Axes of the slice: x: 4, y: 4 (y_hi: 2, y_lo: 2; y = y_hi * 2 + y_lo), z: 16, core: 2. Of those that a mesh axis runs over, the one named last changes fastest.
Arguments:
- queries: bfloat16 [32768, 8192], P(('seq', 'head')), may hold values from -42.5 to 42.5
- key_states: bfloat16 [32768, 1024], P(('seq', 'head')), may hold values from -4 to 4
- value_states: bfloat16 [32768, 1024], P(('seq', 'head')), may hold values from -4 to 4
- out_grads: bfloat16 [32768, 8192], P(('seq', 'head')), may hold values from -4 to 4
- segment_ids: int32 [32768], replicated, may hold values from 0 to 7, as said below
Outputs:
- query_grads: float32 [32768, 8192], P(('seq', 'head'))
- key_grads: float32 [32768, 1024], P(('seq', 'head'))
- value_grads: float32 [32768, 1024], P(('seq', 'head'))
Inputs may be any that keep to these rules, and one draw needn't show every extreme that they name: `segment_ids`: document ids never fall along positions and every one of the 8 documents has at least one position; the last document, 7, holds exactly the positions from 15872 to the end.
All inputs are finite; a program needn't handle non-finite values.
Results may differ from a plain program's by a relative error of at most 0.025.
Values may be sent and summed in bfloat16 or wider, within the bound.
No kernel may reach another device: no remote copies, remote signals or barrier semaphores. Data moves between devices by JAX's collectives and lax.ppermute only.
A program may use at most 64 MiB of HBM per device.

v0:
```python
import math

import jax
import jax.numpy as jnp
from jax import lax
from jax.sharding import PartitionSpec as P

HQ = 64
HK = 8
DH = 128
STRETCH = 256


neg_fill = -1e30


def from_behind(array, axis, by):
    devices = lax.axis_size(axis)
    return lax.ppermute(array, axis, [(i, (i + by) % devices) for i in range(devices)])


def pair_layout(pair_index, pair_count, segment_ids):
    offsets = jnp.arange(STRETCH, dtype=jnp.int32)
    first_start = pair_index * STRETCH
    second_start = (2 * pair_count - 1 - pair_index) * STRETCH
    positions = jnp.concatenate([first_start + offsets, second_start + offsets])
    documents = jnp.concatenate(
        [
            lax.dynamic_slice_in_dim(segment_ids, first_start, STRETCH, 0),
            lax.dynamic_slice_in_dim(segment_ids, second_start, STRETCH, 0),
        ]
    )
    return (positions, documents)


def attend(query_block, grad_block, key_block, value_block, allowed, factor):
    scores = (
        jnp.einsum("rhd,kd->hrk", query_block, key_block, preferred_element_type=jnp.float32)
        * factor
    )
    scores = jnp.where(allowed[None], scores, neg_fill)
    row_peak = jnp.max(scores, axis=2, keepdims=True)
    log_total = row_peak + jnp.log(jnp.sum(jnp.exp(scores - row_peak), axis=2, keepdims=True))
    weights = jnp.where(allowed[None], jnp.exp(scores - log_total), 0.0)
    weights_low = weights.astype(jnp.bfloat16)
    output = jnp.einsum("hrk,kd->rhd", weights_low, value_block, preferred_element_type=jnp.float32)
    row_delta = jnp.sum(grad_block.astype(jnp.float32) * output, axis=2)
    weight_grads = jnp.einsum(
        "rhd,kd->hrk", grad_block, value_block, preferred_element_type=jnp.float32
    )
    score_grads = (weights * (weight_grads - row_delta.T[:, :, None])).astype(jnp.bfloat16)
    query_part = (
        jnp.einsum("hrk,kd->rhd", score_grads, key_block, preferred_element_type=jnp.float32)
        * factor
    )
    key_part = (
        jnp.einsum("hrk,rhd->kd", score_grads, query_block, preferred_element_type=jnp.float32)
        * factor
    )
    value_part = jnp.einsum(
        "hrk,rhd->kd", weights_low, grad_block, preferred_element_type=jnp.float32
    )
    return (query_part, key_part, value_part)


def on_device(queries, key_states, value_states, out_grads, segment_ids):
    local_rows = queries.shape[0]
    group_size = HQ // HK
    factor = 1.0 / math.sqrt(DH)
    pair_span = 2 * STRETCH
    query_heads = queries.reshape(local_rows, HQ, DH)
    grad_heads = out_grads.reshape(local_rows, HQ, DH)
    key_heads = key_states.reshape(local_rows, HK, DH)
    value_heads = value_states.reshape(local_rows, HK, DH)
    query_local, grad_local, key_local, value_local = (
        lax.all_to_all(query_heads, "head", split_axis=1, concat_axis=0, tiled=True),
        lax.all_to_all(grad_heads, "head", split_axis=1, concat_axis=0, tiled=True),
        lax.all_to_all(key_heads, "head", split_axis=1, concat_axis=0, tiled=True),
        lax.all_to_all(value_heads, "head", split_axis=1, concat_axis=0, tiled=True),
    )
    key_prior, value_prior = from_behind((key_local, value_local), "seq", 1)
    pair_count = lax.axis_size("seq")
    seq_index = lax.axis_index("seq")
    prior_pair = (seq_index + pair_count - 1) % pair_count
    own_positions, own_documents = pair_layout(seq_index, pair_count, segment_ids)
    prior_positions, prior_documents = pair_layout(prior_pair, pair_count, segment_ids)
    key_positions = jnp.concatenate([own_positions, prior_positions])
    key_documents = jnp.concatenate([own_documents, prior_documents])
    allowed = (key_positions[None, :] <= own_positions[:, None]) & (
        key_documents[None, :] == own_documents[:, None]
    )
    local_heads = query_local.shape[1]
    local_groups = key_local.shape[1]
    key_all = jnp.concatenate([key_local, key_prior], axis=0)
    value_all = jnp.concatenate([value_local, value_prior], axis=0)

    def block_step(running, block_index):
        key_acc, value_acc = running
        head_first = block_index * 2
        group_index = head_first // group_size
        query_block = lax.dynamic_slice_in_dim(query_local, head_first, 2, 1)
        grad_block = lax.dynamic_slice_in_dim(grad_local, head_first, 2, 1)
        key_block = lax.dynamic_index_in_dim(key_all, group_index, 1, keepdims=False)
        value_block = lax.dynamic_index_in_dim(value_all, group_index, 1, keepdims=False)
        query_part, key_part, value_part = attend(
            query_block, grad_block, key_block, value_block, allowed, factor
        )
        key_slot = lax.dynamic_index_in_dim(key_acc, group_index, 1, keepdims=False) + key_part
        value_slot = (
            lax.dynamic_index_in_dim(value_acc, group_index, 1, keepdims=False) + value_part
        )
        key_acc = lax.dynamic_update_index_in_dim(key_acc, key_slot, group_index, 1)
        value_acc = lax.dynamic_update_index_in_dim(value_acc, value_slot, group_index, 1)
        return ((key_acc, value_acc), query_part)

    zero_grads = jnp.zeros((2 * pair_span, local_groups, DH), jnp.float32)
    (key_acc, value_acc), query_parts = lax.scan(
        block_step, (zero_grads, zero_grads), jnp.arange(local_heads // 2, dtype=jnp.int32)
    )
    query_grad = jnp.moveaxis(query_parts, 0, 1).reshape(pair_span, local_heads, DH)
    key_own = key_acc[:pair_span]
    value_own = value_acc[:pair_span]
    key_far = key_acc[pair_span:]
    value_far = value_acc[pair_span:]
    key_back, value_back = from_behind((key_far, value_far), "seq", -1)
    query_out, key_out, value_out = (
        lax.all_to_all(query_grad, "head", split_axis=0, concat_axis=1, tiled=True),
        lax.all_to_all(key_own + key_back, "head", split_axis=0, concat_axis=1, tiled=True),
        lax.all_to_all(value_own + value_back, "head", split_axis=0, concat_axis=1, tiled=True),
    )
    return (
        query_out.reshape(local_rows, HQ * DH),
        key_out.reshape(local_rows, HK * DH),
        value_out.reshape(local_rows, HK * DH),
    )


def solution(mesh):
    return jax.shard_map(
        on_device,
        mesh=mesh,
        in_specs=(
            P(("seq", "head"), None),
            P(("seq", "head"), None),
            P(("seq", "head"), None),
            P(("seq", "head"), None),
            P(),
        ),
        out_specs=(P(("seq", "head"), None), P(("seq", "head"), None), P(("seq", "head"), None)),
        check_vma=False,
    )
```

profile of v0, /device:TPU:1, one launch (start us, length us, event | category | flops | bytes accessed | tf_op | source)
XLA Modules:
  0.0 198.7 jit_solution(7304364860661125517)
XLA Ops:
  0.7 1.7 copy_bitcast_fusion.6
  2.4 7.5 %all-to-all-start.1 = ((bf16[64,8,128]{2,0,1:T(8,128)(2,1)}), bf16[64,8,128]{2,0,1:T(8,128)(2,1)S(1)}, u32[]{:S(2)}, u32[]{:S(2)}) async-start(bf16[64,8,128]{2,0,1:T(8,128)(2,1)} %copy_bitcast_fusion.6), calls=%async_computation.1 | async-start | bytes 262144 | tf_op jit(solution)/shard_map/all_to_all | solution.py:78
  9.9 1.6 copy_bitcast_fusion.5
  11.4 5.2 %all-to-all-done.1 = bf16[64,8,128]{2,0,1:T(8,128)(2,1)S(1)} async-done(((bf16[64,8,128]{2,0,1:T(8,128)(2,1)}), bf16[64,8,128]{2,0,1:T(8,128)(2,1)S(1)}, u32[]{:S(2)}, u32[]{:S(2)}) %all-to-all-start.1) | async-done | bytes 131104 | tf_op jit(solution)/shard_map/all_to_all | solution.py:78
  16.6 3.4 %all-to-all-start.3 = ((bf16[64,8,128]{2,0,1:T(8,128)(2,1)}), bf16[64,8,128]{2,0,1:T(8,128)(2,1)S(1)}, u32[]{:S(2)}, u32[]{:S(2)}) async-start(bf16[64,8,128]{2,0,1:T(8,128)(2,1)} %copy_bitcast_fusion.5), calls=%async_computation.3 | async-start | bytes 262144 | tf_op jit(solution)/shard_map/all_to_all | solution.py:79
  20.0 1.3 copy_bitcast_fusion.2
  21.3 5.4 %all-to-all-done.3 = bf16[64,8,128]{2,0,1:T(8,128)(2,1)S(1)} async-done(((bf16[64,8,128]{2,0,1:T(8,128)(2,1)}), bf16[64,8,128]{2,0,1:T(8,128)(2,1)S(1)}, u32[]{:S(2)}, u32[]{:S(2)}) %all-to-all-start.3) | async-done | bytes 131104 | tf_op jit(solution)/shard_map/all_to_all | solution.py:79
  26.7 3.6 %all-to-all-start = ((bf16[64,64,128]{2,0,1:T(8,128)(2,1)}), bf16[64,64,128]{2,0,1:T(8,128)(2,1)S(1)}, u32[]{:S(2)}, u32[]{:S(2)}) async-start(bf16[64,64,128]{2,0,1:T(8,128)(2,1)} %copy_bitcast_fusion.2), calls=%async_computation | async-start | bytes 2097152 | tf_op jit(solution)/shard_map/all_to_all | solution.py:76
  30.3 1.3 copy_bitcast_fusion.1
  31.6 9.7 %all-to-all-done = bf16[64,64,128]{2,0,1:T(8,128)(2,1)S(1)} async-done(((bf16[64,64,128]{2,0,1:T(8,128)(2,1)}), bf16[64,64,128]{2,0,1:T(8,128)(2,1)S(1)}, u32[]{:S(2)}, u32[]{:S(2)}) %all-to-all-start) | async-done | bytes 1048608 | tf_op jit(solution)/shard_map/all_to_all | solution.py:76
  41.3 4.2 %all-to-all-start.2 = ((bf16[64,64,128]{2,0,1:T(8,128)(2,1)}), bf16[64,64,128]{2,0,1:T(8,128)(2,1)}, u32[]{:S(2)}, u32[]{:S(2)}) async-start(bf16[64,64,128]{2,0,1:T(8,128)(2,1)} %copy_bitcast_fusion.1), calls=%async_computation.2 | async-start | bytes 2097152 | tf_op jit(solution)/shard_map/all_to_all | solution.py:77
  45.6 0.9 fusion.31
  46.5 9.5 %collective-permute-start.1 = (bf16[512,1,128]{2,0,1:T(8,128)(2,1)S(1)}, bf16[512,1,128]{2,0,1:T(8,128)(2,1)S(1)}, u32[]{:S(2)}, u32[]{:S(2)}) collective-permute-start(bf16[512,1,128]{2,0,1:T(8,128)(2,1)S(1)} %bitcast.206), channel_id=1, source_target_pairs={{0,1},{1,2},{2,3},{3,4},{4,5},{5,6},{6,7},{7,8},{8,9},{9,10},{10,1... | collective-permute-start | bytes 393224 | tf_op jit(solution)/shard_map/ppermute | solution.py:19
  56.0 1.9 collective-permute-start
  58.0 0.9 copy.75
  58.8 1.0 collective-permute-done
  60.6 2.9 %copy.71 = bf16[8,64,8,128]{3,2,1,0:T(8,128)(2,1)} copy(bf16[8,64,8,128]{3,1,2,0:T(8,128)(2,1)} %bitcast.11) | data formatting | bytes 2097152 | tf_op jit(solution)/shard_map/all_to_all | solution.py:77
  63.5 0.8 broadcast_in_dim.46.clone
  64.4 55.7 %while.15 = (s32[]{:T(128)}, f32[1024,1,128]{2,0,1:T(8,128)S(1)}, f32[1024,1,128]{2,0,1:T(8,128)}, f32[4,512,2,128]{3,1,2,0:T(8,128)}, s32[4]{0:T(128)S(1)}, /*i...) while((s32[]{:T(128)}, f32[1024,1,128]{2,0,1:T(8,128)S(1)}, ...), condition=%wide.region_4.5_spmd.clone, body=%wide.region_0.4_spmd.clone.sunk | while | flops 1638266880 | bytes 41738552 | solution.py:117
  65.6 1.8 constant_dynamic-slice_fusion.3
  67.9 1.1 bitcast_reduce_fusion.2
  69.0 1.2 fusion.64
  70.3 1.6 fusion.65
  71.9 1.9 fusion.68
  73.8 2.1 %fusion.66 = bf16[2,512,1024]{2,1,0:T(8,128)(2,1)S(1)} fusion(f32[512,2,1024]{2,0,1:T(8,128)S(1)} %get-tuple-element.270, f32[2,512]{1,0:T(2,128)S(1)} %bitcast.211, f32[2,512]{1,0:T(2,128)S(1)} %log_add_fusion.2, pred[512,1024]{1,0:T(8,128)(4,1)S(1)} %compare_and_fusion.2, bf16[1024,1,128]{0,2,1:T(8,128)(2,1)S(1)} %copy-done.5, ...), kind=kOutput, calls=%fused_computation.3.clone.1 | convolution fusion | flops 275775488 | bytes 7348224 | tf_op jit(solution)/shard_map/while/body/eval_jaxpr/rhd,kd->hrk/dot_general | solution.py:48
  76.8 1.5 fusion.69
  79.6 1.8 constant_dynamic-slice_fusion.3
  81.8 1.1 bitcast_reduce_fusion.2
  83.0 1.2 fusion.64
  84.2 1.6 fusion.65
  85.8 1.9 fusion.68
  87.7 2.1 %fusion.66 = bf16[2,512,1024]{2,1,0:T(8,128)(2,1)S(1)} fusion(f32[512,2,1024]{2,0,1:T(8,128)S(1)} %get-tuple-element.270, f32[2,512]{1,0:T(2,128)S(1)} %bitcast.211, f32[2,512]{1,0:T(2,128)S(1)} %log_add_fusion.2, pred[512,1024]{1,0:T(8,128)(4,1)S(1)} %compare_and_fusion.2, bf16[1024,1,128]{0,2,1:T(8,128)(2,1)S(1)} %copy-done.5, ...), kind=kOutput, calls=%fused_computation.3.clone.1 | convolution fusion | flops 275775488 | bytes 7348224 | tf_op jit(solution)/shard_map/while/body/eval_jaxpr/rhd,kd->hrk/dot_general | solution.py:48
  89.9 0.8 fusion.67
  90.7 1.5 fusion.69
  93.5 1.8 constant_dynamic-slice_fusion.3
  95.8 1.1 bitcast_reduce_fusion.2
  96.9 1.2 fusion.64
  98.1 1.6 fusion.65
  99.7 1.9 fusion.68
  101.7 2.1 %fusion.66 = bf16[2,512,1024]{2,1,0:T(8,128)(2,1)S(1)} fusion(f32[512,2,1024]{2,0,1:T(8,128)S(1)} %get-tuple-element.270, f32[2,512]{1,0:T(2,128)S(1)} %bitcast.211, f32[2,512]{1,0:T(2,128)S(1)} %log_add_fusion.2, pred[512,1024]{1,0:T(8,128)(4,1)S(1)} %compare_and_fusion.2, bf16[1024,1,128]{0,2,1:T(8,128)(2,1)S(1)} %copy-done.5, ...), kind=kOutput, calls=%fused_computation.3.clone.1 | convolution fusion | flops 275775488 | bytes 7348224 | tf_op jit(solution)/shard_map/while/body/eval_jaxpr/rhd,kd->hrk/dot_general | solution.py:48
  103.8 0.8 fusion.67
  104.6 1.5 fusion.69
  107.4 1.8 constant_dynamic-slice_fusion.3
  109.7 1.1 bitcast_reduce_fusion.2
  110.8 1.2 fusion.64
  112.1 1.6 fusion.65
  113.7 1.9 fusion.68
  115.6 2.1 %fusion.66 = bf16[2,512,1024]{2,1,0:T(8,128)(2,1)S(1)} fusion(f32[512,2,1024]{2,0,1:T(8,128)S(1)} %get-tuple-element.270, f32[2,512]{1,0:T(2,128)S(1)} %bitcast.211, f32[2,512]{1,0:T(2,128)S(1)} %log_add_fusion.2, pred[512,1024]{1,0:T(8,128)(4,1)S(1)} %compare_and_fusion.2, bf16[1024,1,128]{0,2,1:T(8,128)(2,1)S(1)} %copy-done.5, ...), kind=kOutput, calls=%fused_computation.3.clone.1 | convolution fusion | flops 275775488 | bytes 7348224 | tf_op jit(solution)/shard_map/while/body/eval_jaxpr/rhd,kd->hrk/dot_general | solution.py:48
  117.8 0.8 fusion.67
  118.6 1.5 fusion.69
  120.1 9.4 %collective-permute-start.2 = (f32[512,1,128]{2,1,0:T(1,128)S(1)}, f32[512,1,128]{2,1,0:T(1,128)S(1)}, u32[]{:S(2)}, u32[]{:S(2)}) collective-permute-start(f32[512,1,128]{2,1,0:T(1,128)S(1)} %bitcast.210), channel_id=1, source_target_pairs={{0,63},{1,0},{2,1},{3,2},{4,3},{5,4},{6,5},{7,6},{8,7},{9,8},{10,9... | collective-permute-start | bytes 786440 | tf_op jit(solution)/shard_map/ppermute | solution.py:19
  129.6 1.8 fusion.29
  131.4 8.5 %collective-permute-start.3 = (f32[512,1,128]{2,1,0:T(1,128)}, f32[512,1,128]{2,1,0:T(1,128)}, u32[]{:S(2)}, u32[]{:S(2)}) collective-permute-start(f32[512,1,128]{2,1,0:T(1,128)} %bitcast.27), channel_id=1, source_target_pairs={{0,63},{1,0},{2,1},{3,2},{4,3},{5,4},{6,5},{7,6},{8,7},{9,8},{10,9... | collective-permute-start | bytes 786440 | tf_op jit(solution)/shard_map/ppermute | solution.py:19
  140.0 1.0 add.94
  141.0 5.0 %all-to-all-start.5 = ((f32[512,1,128]{2,1,0:T(1,128)}), f32[512,1,128]{2,1,0:T(1,128)S(1)}, u32[]{:S(2)}, u32[]{:S(2)}) async-start(f32[512,1,128]{2,1,0:T(1,128)} %add.94), calls=%async_computation.5 | async-start | bytes 524288 | tf_op jit(solution)/shard_map/all_to_all | solution.py:128
  146.0 2.0 %add.95 = f32[512,1,128]{2,1,0:T(1,128)} add(f32[512,1,128]{2,1,0:T(1,128)} %bitcast.200, f32[512,1,128]{2,1,0:T(1,128)} %collective-permute-done.3) | non-fusion elementwise | flops 65536 | bytes 786432 | tf_op jit(solution)/shard_map/add | solution.py:129
  148.0 5.3 %all-to-all-done.5 = f32[512,1,128]{2,1,0:T(1,128)S(1)} async-done(((f32[512,1,128]{2,1,0:T(1,128)}), f32[512,1,128]{2,1,0:T(1,128)S(1)}, u32[]{:S(2)}, u32[]{:S(2)}) %all-to-all-start.5) | async-done | bytes 262176 | tf_op jit(solution)/shard_map/all_to_all | solution.py:128
  153.3 4.0 %all-to-all-start.6 = ((f32[512,1,128]{2,1,0:T(1,128)}), f32[512,1,128]{2,1,0:T(1,128)}, u32[]{:S(2)}, u32[]{:S(2)}) async-start(f32[512,1,128]{2,1,0:T(1,128)} %add.95), calls=%async_computation.6 | async-start | bytes 524288 | tf_op jit(solution)/shard_map/all_to_all | solution.py:129
  157.4 2.9 %copy.76 = f32[512,4,2,128]{3,2,1,0:T(2,128)} copy(f32[512,4,2,128]{3,0,2,1:T(8,128)S(1)} %bitcast.197) | data formatting | bytes 4194304 | tf_op jit(solution)/shard_map/transpose | solution.py:120
  160.3 4.4 %all-to-all-done.6 = f32[512,1,128]{2,1,0:T(1,128)} async-done(((f32[512,1,128]{2,1,0:T(1,128)}), f32[512,1,128]{2,1,0:T(1,128)}, u32[]{:S(2)}, u32[]{:S(2)}) %all-to-all-start.6) | async-done | bytes 262176 | tf_op jit(solution)/shard_map/all_to_all | solution.py:129
  164.7 3.6 %all-to-all-start.4 = ((f32[512,8,128]{2,1,0:T(8,128)}), f32[512,8,128]{2,1,0:T(8,128)S(1)}, u32[]{:S(2)}, u32[]{:S(2)}) async-start(f32[512,8,128]{2,1,0:T(8,128)} %bitcast.19), calls=%async_computation.4 | async-start | bytes 4194304 | tf_op jit(solution)/shard_map/all_to_all | solution.py:127
  169.2 1.1 copy.83
  171.1 24.8 %all-to-all-done.4 = f32[512,8,128]{2,1,0:T(8,128)S(1)} async-done(((f32[512,8,128]{2,1,0:T(8,128)}), f32[512,8,128]{2,1,0:T(8,128)S(1)}, u32[]{:S(2)}, u32[]{:S(2)}) %all-to-all-start.4) | async-done | bytes 2097184 | tf_op jit(solution)/shard_map/all_to_all | solution.py:127
  196.2 2.5 %copy.118 = f32[8,8,64,128]{3,1,2,0:T(8,128)} copy(f32[8,8,64,128]{3,2,1,0:T(8,128)S(1)} %bitcast.193) | data formatting | bytes 4194304
  (64 shorter events, 8.1 us)
Async XLA Ops:
  0.6 19.4 %copy-start = (bf16[64,8192]{1,0:T(8,128)(2,1)S(1)}, bf16[64,8192]{1,0:T(8,128)(2,1)}, u32[]{:S(2)}) copy-start(bf16[64,8192]{1,0:T(8,128)(2,1)} %param.7) | copy-start | bytes 3145732
  0.6 29.6 %copy-start.4 = (bf16[64,8192]{1,0:T(8,128)(2,1)S(1)}, bf16[64,8192]{1,0:T(8,128)(2,1)}, u32[]{:S(2)}) copy-start(bf16[64,8192]{1,0:T(8,128)(2,1)} %param.10) | copy-start | bytes 3145732
  2.4 14.2 %all-to-all-start.1 = ((bf16[64,8,128]{2,0,1:T(8,128)(2,1)}), bf16[64,8,128]{2,0,1:T(8,128)(2,1)S(1)}, u32[]{:S(2)}, u32[]{:S(2)}) async-start(bf16[64,8,128]{2,0,1:T(8,128)(2,1)} %copy_bitcast_fusion.6), calls=%async_computation.1 | async-start | bytes 262144 | tf_op jit(solution)/shard_map/all_to_all | solution.py:78
  16.6 10.1 %all-to-all-start.3 = ((bf16[64,8,128]{2,0,1:T(8,128)(2,1)}), bf16[64,8,128]{2,0,1:T(8,128)(2,1)S(1)}, u32[]{:S(2)}, u32[]{:S(2)}) async-start(bf16[64,8,128]{2,0,1:T(8,128)(2,1)} %copy_bitcast_fusion.5), calls=%async_computation.3 | async-start | bytes 262144 | tf_op jit(solution)/shard_map/all_to_all | solution.py:79
  26.7 14.6 %all-to-all-start = ((bf16[64,64,128]{2,0,1:T(8,128)(2,1)}), bf16[64,64,128]{2,0,1:T(8,128)(2,1)S(1)}, u32[]{:S(2)}, u32[]{:S(2)}) async-start(bf16[64,64,128]{2,0,1:T(8,128)(2,1)} %copy_bitcast_fusion.2), calls=%async_computation | async-start | bytes 2097152 | tf_op jit(solution)/shard_map/all_to_all | solution.py:76
  41.3 19.3 %all-to-all-start.2 = ((bf16[64,64,128]{2,0,1:T(8,128)(2,1)}), bf16[64,64,128]{2,0,1:T(8,128)(2,1)}, u32[]{:S(2)}, u32[]{:S(2)}) async-start(bf16[64,64,128]{2,0,1:T(8,128)(2,1)} %copy_bitcast_fusion.1), calls=%async_computation.2 | async-start | bytes 2097152 | tf_op jit(solution)/shard_map/all_to_all | solution.py:77
  46.5 11.5 %collective-permute-start.1 = (bf16[512,1,128]{2,0,1:T(8,128)(2,1)S(1)}, bf16[512,1,128]{2,0,1:T(8,128)(2,1)S(1)}, u32[]{:S(2)}, u32[]{:S(2)}) collective-permute-start(bf16[512,1,128]{2,0,1:T(8,128)(2,1)S(1)} %bitcast.206), channel_id=1, source_target_pairs={{0,1},{1,2},{2,3},{3,4},{4,5},{5,6},{6,7},{7,8},{8,9},{9,10},{10,1... | collective-permute-start | bytes 393224 | tf_op jit(solution)/shard_map/ppermute | solution.py:19
  56.0 3.9 %collective-permute-start = (bf16[512,1,128]{2,0,1:T(8,128)(2,1)S(1)}, bf16[512,1,128]{2,0,1:T(8,128)(2,1)S(1)}, u32[]{:S(2)}, u32[]{:S(2)}) collective-permute-start(bf16[512,1,128]{2,0,1:T(8,128)(2,1)S(1)} %bitcast.204), channel_id=1, source_target_pairs={{0,1},{1,2},{2,3},{3,4},{4,5},{5,6},{6,7},{7,8},{8,9},{9,10},{10,1... | collective-permute-start | bytes 393224 | tf_op jit(solution)/shard_map/ppermute | solution.py:19
  67.9 2.4 %copy-start.5 = (bf16[1024,1,128]{0,2,1:T(8,128)(2,1)S(1)}, bf16[1024,1,128]{0,2,1:T(8,128)(2,1)}, u32[]{:S(2)}) copy-start(bf16[1024,1,128]{0,2,1:T(8,128)(2,1)} %get-tuple-element.315) | copy-start | bytes 786436 | tf_op jit(solution)/shard_map/while
  70.3 1.6 copy-start.2
  73.8 2.2 %copy-start.3 = (f32[1024,1,128]{2,0,1:T(8,128)}, f32[1024,1,128]{2,0,1:T(8,128)S(1)}, u32[]{:S(2)}) copy-start(f32[1024,1,128]{2,0,1:T(8,128)S(1)} %fusion.68) | copy-start | bytes 1572868 | tf_op jit(solution)/shard_map/while
  81.8 2.4 %copy-start.5 = (bf16[1024,1,128]{0,2,1:T(8,128)(2,1)S(1)}, bf16[1024,1,128]{0,2,1:T(8,128)(2,1)}, u32[]{:S(2)}) copy-start(bf16[1024,1,128]{0,2,1:T(8,128)(2,1)} %get-tuple-element.315) | copy-start | bytes 786436 | tf_op jit(solution)/shard_map/while
  84.2 1.6 copy-start.2
  87.7 2.2 %copy-start.3 = (f32[1024,1,128]{2,0,1:T(8,128)}, f32[1024,1,128]{2,0,1:T(8,128)S(1)}, u32[]{:S(2)}) copy-start(f32[1024,1,128]{2,0,1:T(8,128)S(1)} %fusion.68) | copy-start | bytes 1572868 | tf_op jit(solution)/shard_map/while
  95.8 2.4 %copy-start.5 = (bf16[1024,1,128]{0,2,1:T(8,128)(2,1)S(1)}, bf16[1024,1,128]{0,2,1:T(8,128)(2,1)}, u32[]{:S(2)}) copy-start(bf16[1024,1,128]{0,2,1:T(8,128)(2,1)} %get-tuple-element.315) | copy-start | bytes 786436 | tf_op jit(solution)/shard_map/while
  98.1 1.6 copy-start.2
  101.7 2.2 %copy-start.3 = (f32[1024,1,128]{2,0,1:T(8,128)}, f32[1024,1,128]{2,0,1:T(8,128)S(1)}, u32[]{:S(2)}) copy-start(f32[1024,1,128]{2,0,1:T(8,128)S(1)} %fusion.68) | copy-start | bytes 1572868 | tf_op jit(solution)/shard_map/while
  109.7 2.4 %copy-start.5 = (bf16[1024,1,128]{0,2,1:T(8,128)(2,1)S(1)}, bf16[1024,1,128]{0,2,1:T(8,128)(2,1)}, u32[]{:S(2)}) copy-start(bf16[1024,1,128]{0,2,1:T(8,128)(2,1)} %get-tuple-element.315) | copy-start | bytes 786436 | tf_op jit(solution)/shard_map/while
  112.0 1.6 copy-start.2
  115.6 2.2 %copy-start.3 = (f32[1024,1,128]{2,0,1:T(8,128)}, f32[1024,1,128]{2,0,1:T(8,128)S(1)}, u32[]{:S(2)}) copy-start(f32[1024,1,128]{2,0,1:T(8,128)S(1)} %fusion.68) | copy-start | bytes 1572868 | tf_op jit(solution)/shard_map/while
  120.1 37.2 %copy-start.1 = (f32[4,512,2,128]{3,1,2,0:T(8,128)S(1)}, f32[4,512,2,128]{3,1,2,0:T(8,128)}, u32[]{:S(2)}) copy-start(f32[4,512,2,128]{3,1,2,0:T(8,128)} %get-tuple-element.57) | copy-start | bytes 6291460
  120.1 19.8 %collective-permute-start.2 = (f32[512,1,128]{2,1,0:T(1,128)S(1)}, f32[512,1,128]{2,1,0:T(1,128)S(1)}, u32[]{:S(2)}, u32[]{:S(2)}) collective-permute-start(f32[512,1,128]{2,1,0:T(1,128)S(1)} %bitcast.210), channel_id=1, source_target_pairs={{0,63},{1,0},{2,1},{3,2},{4,3},{5,4},{6,5},{7,6},{8,7},{9,8},{10,9... | collective-permute-start | bytes 786440 | tf_op jit(solution)/shard_map/ppermute | solution.py:19
  131.4 14.6 %collective-permute-start.3 = (f32[512,1,128]{2,1,0:T(1,128)}, f32[512,1,128]{2,1,0:T(1,128)}, u32[]{:S(2)}, u32[]{:S(2)}) collective-permute-start(f32[512,1,128]{2,1,0:T(1,128)} %bitcast.27), channel_id=1, source_target_pairs={{0,63},{1,0},{2,1},{3,2},{4,3},{5,4},{6,5},{7,6},{8,7},{9,8},{10,9... | collective-permute-start | bytes 786440 | tf_op jit(solution)/shard_map/ppermute | solution.py:19
  141.0 12.3 %all-to-all-start.5 = ((f32[512,1,128]{2,1,0:T(1,128)}), f32[512,1,128]{2,1,0:T(1,128)S(1)}, u32[]{:S(2)}, u32[]{:S(2)}) async-start(f32[512,1,128]{2,1,0:T(1,128)} %add.94), calls=%async_computation.5 | async-start | bytes 524288 | tf_op jit(solution)/shard_map/all_to_all | solution.py:128
  153.3 11.4 %all-to-all-start.6 = ((f32[512,1,128]{2,1,0:T(1,128)}), f32[512,1,128]{2,1,0:T(1,128)}, u32[]{:S(2)}, u32[]{:S(2)}) async-start(f32[512,1,128]{2,1,0:T(1,128)} %add.95), calls=%async_computation.6 | async-start | bytes 524288 | tf_op jit(solution)/shard_map/all_to_all | solution.py:129
  164.7 31.2 %all-to-all-start.4 = ((f32[512,8,128]{2,1,0:T(8,128)}), f32[512,8,128]{2,1,0:T(8,128)S(1)}, u32[]{:S(2)}, u32[]{:S(2)}) async-start(f32[512,8,128]{2,1,0:T(8,128)} %bitcast.19), calls=%async_computation.4 | async-start | bytes 4194304 | tf_op jit(solution)/shard_map/all_to_all | solution.py:127
where the time goes:
time: 200 us; the launch traced here: 199 us
  starting transfers between devices  60.7 us (30%)
  waiting for transfers between devices  55.8 us (28%)
  matrix products  36.5 us (18%)
  local copies, waits for them, and re-layouts  32 us (16%)
  other arithmetic  9.84 us (5%)
  loops' own time  2.91 us (1%)
    ppermute x4, starting transfers between devices, from_behind(): lax.ppermute(array, axis, [(i, (i + by) % devices) for i in range(devices)])  29.4 us
    all_to_all x1, waiting for transfers between devices, on_device(): lax.all_to_all(query_grad, 'head', split_axis=0, concat_axis=1, tiled=True)  24.8 us
    all_to_all x1, waiting for transfers between devices, on_device(): lax.all_to_all(query_heads, 'head', split_axis=1, concat_axis=0, tiled=True)  9.7 us
    dot_general x4, matrix products, attend(): jnp.einsum('rhd,kd->hrk', grad_block, value_block, preferred_element_type...  8.58 us
    dot_general x4, matrix products, attend(): jnp.einsum('hrk,rhd->kd', weights_low, grad_block, preferred_element_type...  7.66 us
    all_to_all x1, starting transfers between devices, on_device(): lax.all_to_all(key_heads, 'head', split_axis=1, concat_axis=0, tiled=True)  7.48 us
    dynamic_slice x4, local copies, waits for them, and re-layouts, block_step(): grad_block = lax.dynamic_slice_in_dim(grad_local, head_first, 2, 1)  7.09 us
    dot_general x4, matrix products, attend(): jnp.einsum('hrk,kd->rhd', weights_low, value_block, preferred_element_typ...  6.43 us
  transfers between devices with their start and end apart: 11, of which 7 were waited for; matrix products, arithmetic and copies ran while one was open for 9% of the time, Pallas kernels for 0%

commit v1 on v0

v1 whole, which is shorter than its diff:
```python
import math

import jax
import jax.numpy as jnp
from jax import lax
from jax.experimental import pallas as pl
from jax.experimental.pallas import tpu as pltpu
from jax.sharding import Mesh, PartitionSpec as P

HQ = 64
HK = 8
DH = 128
STRETCH = 256
GROUP = HQ // HK
PAIRS = 64
ROWS = 64

FACTOR = 1.0 / math.sqrt(DH)
LOG2E = 1.4426950408889634
FILL = -1e30

TEAM = ("core", "xl", "yh")
CHAIN = ("xh", "yl", "z")

OWN0, OWN1, FROM_PREV, EXTRA0, EXTRA1 = (i * STRETCH for i in range(5))


def chain_pairs():
    last = PAIRS // 2 - 1
    late = PAIRS // 2
    forward = [(n, n + 1) for n in range(last)] + [(last, late)]
    extra = [(last, late + last), (late + last, late)]
    return forward, extra


def back(pairs):
    return [(b, a) for a, b in pairs]


def nt_dot(a, b):
    return lax.dot_general(a, b, (((1,), (1,)), ((), ())), preferred_element_type=jnp.float32)


def nn_dot(a, b):
    return lax.dot_general(a, b, (((1,), (0,)), ((), ())), preferred_element_type=jnp.float32)


def attend_kernel(
    spot_ref, rows_ref, own_ref, prev_ref, extra_ref, seg_ref,
    dq_ref, down_ref, dprev_ref, dextra_ref,
    kv, kt, acc, bias,
):
    late = spot_ref[0]
    n = spot_ref[1]
    last = PAIRS // 2 - 1
    kv[0:512, :] = own_ref[...]
    kv[512:768, :] = prev_ref[...]
    kv[768:1280, :] = extra_ref[...]
    acc[...] = jnp.zeros_like(acc)
    kt[...] = kv[:, 0:DH].astype(jnp.float32).T.astype(jnp.bfloat16)

    def block_of(pair, is_late):
        return jnp.where(is_late == 1, 2 * PAIRS - 1 - pair, pair)

    def fill_bias(place, q_block, k_block):
        q_doc = jnp.broadcast_to(seg_ref[pl.ds(q_block, 1), :], (STRETCH, STRETCH))
        k_doc = jnp.broadcast_to(seg_ref[pl.ds(k_block, 1), :], (STRETCH, STRETCH))
        k_doc = k_doc.astype(jnp.float32).T
        k_pos = k_block * STRETCH + lax.broadcasted_iota(jnp.int32, (STRETCH, STRETCH), 0)
        q_pos = q_block * STRETCH + lax.broadcasted_iota(jnp.int32, (STRETCH, STRETCH), 1)
        ok = (k_pos <= q_pos) & (k_doc == q_doc.astype(jnp.float32))
        bias[place] = jnp.where(ok, 0.0, FILL)

    def run(q_base, q_block, offsets, blocks):
        count = len(offsets)
        for i in range(count):
            fill_bias(i, q_block, blocks[i])

        @pl.loop(0, GROUP)
        def _(h):
            col = pl.multiple_of(h * DH, DH)
            q = rows_ref[q_base : q_base + STRETCH, pl.ds(col, DH)]
            g = rows_ref[q_base : q_base + STRETCH, pl.ds(GROUP * DH + col, DH)]
            scores = [
                nt_dot(kv[pl.ds(o, STRETCH), 0:DH], q) * (FACTOR * LOG2E) + bias[i]
                for i, o in enumerate(offsets)
            ]
            peak = jnp.max(scores[0], axis=0, keepdims=True)
            for s in scores[1:]:
                peak = jnp.maximum(peak, jnp.max(s, axis=0, keepdims=True))
            exps = [jnp.exp2(s - peak) for s in scores]
            wgrads = [nt_dot(kv[pl.ds(o, STRETCH), DH : 2 * DH], g) for o in offsets]
            total = sum(jnp.sum(e, axis=0, keepdims=True) for e in exps)
            delta = sum(jnp.sum(e * w, axis=0, keepdims=True) for e, w in zip(exps, wgrads))
            inverse = 1.0 / total
            delta = delta * inverse
            dq_t = None
            for o, e, w in zip(offsets, exps, wgrads):
                weights = e * inverse
                score_grads = (weights * (w - delta)).astype(jnp.bfloat16)
                acc[pl.ds(o, STRETCH), 0:DH] += nn_dot(score_grads, q)
                acc[pl.ds(o, STRETCH), DH : 2 * DH] += nn_dot(weights.astype(jnp.bfloat16), g)
                part = nn_dot(kt[:, pl.ds(o, STRETCH)], score_grads)
                dq_t = part if dq_t is None else dq_t + part
            dq_ref[q_base : q_base + STRETCH, pl.ds(col, DH)] = (
                (dq_t * FACTOR).T.astype(jnp.bfloat16)
            )

    pair0 = 2 * n
    pair1 = 2 * n + 1
    b0 = block_of(pair0, late)
    b1 = block_of(pair1, late)
    head = (late == 1) & (n == 0)
    tail = (late == 1) & (n == last)
    early = late == 0
    plain_late = (late == 1) & (n != 0) & (n != last)
    end_early = PAIRS - 1
    end_late = PAIRS

    @pl.when((early & (n == 0)) | plain_late)
    def _():
        run(0, b0, [OWN0], [b0])

    @pl.when((early & (n > 0)) | tail)
    def _():
        off = pl.multiple_of(jnp.where(early, FROM_PREV, EXTRA0), STRETCH)
        run(0, b0, [OWN0, off], [b0, jnp.where(early, pair0 - 1, end_early - 1)])

    @pl.when(head)
    def _():
        run(0, b0, [OWN0, FROM_PREV, EXTRA1], [b0, end_early, end_late])

    @pl.when((late == 1) & (n != last))
    def _():
        run(STRETCH, b1, [OWN1], [b1])

    @pl.when(early)
    def _():
        run(STRETCH, b1, [OWN1, OWN0], [b1, b0])

    @pl.when(tail)
    def _():
        run(STRETCH, b1, [OWN1, EXTRA0, EXTRA1], [b1, end_early - 1, end_early])

    down_ref[:, 0:DH] = acc[0:512, 0:DH] * FACTOR
    down_ref[:, DH : 2 * DH] = acc[0:512, DH : 2 * DH]
    dprev_ref[:, 0:DH] = (acc[512:768, 0:DH] * FACTOR).astype(jnp.bfloat16)
    dprev_ref[:, DH : 2 * DH] = acc[512:768, DH : 2 * DH].astype(jnp.bfloat16)
    dextra_ref[:, 0:DH] = (acc[768:1280, 0:DH] * FACTOR).astype(jnp.bfloat16)
    dextra_ref[:, DH : 2 * DH] = acc[768:1280, DH : 2 * DH].astype(jnp.bfloat16)


def attend(spot, rows, own, prev, extra, seg):
    vmem = pl.BlockSpec(memory_space=pltpu.VMEM)
    return pl.pallas_call(
        attend_kernel,
        out_shape=(
            jax.ShapeDtypeStruct((512, GROUP * DH), jnp.bfloat16),
            jax.ShapeDtypeStruct((512, 2 * DH), jnp.float32),
            jax.ShapeDtypeStruct((256, 2 * DH), jnp.bfloat16),
            jax.ShapeDtypeStruct((512, 2 * DH), jnp.bfloat16),
        ),
        in_specs=[pl.BlockSpec(memory_space=pltpu.SMEM)] + [vmem] * 5,
        out_specs=(vmem,) * 4,
        scratch_shapes=[
            pltpu.VMEM((1280, 2 * DH), jnp.bfloat16),
            pltpu.VMEM((DH, 1280), jnp.bfloat16),
            pltpu.VMEM((1280, 2 * DH), jnp.float32),
            pltpu.VMEM((3, STRETCH, STRETCH), jnp.float32),
        ],
        compiler_params=pltpu.CompilerParams(vmem_limit_bytes=32 * 1024 * 1024),
        cost_estimate=pl.CostEstimate(
            flops=2 * 5 * 4 * 8 * 256 * 256 * 128, bytes_accessed=6 * 2**20,
            transcendentals=4 * 8 * 256 * 256,
        ),
        name="attend",
    )(spot, rows, own, prev, extra, seg)


def on_device(queries, key_states, value_states, out_grads, segment_ids):
    forward, extra = chain_pairs()

    def split_heads(array):
        return jnp.swapaxes(array.reshape(ROWS, HK, -1), 0, 1)

    with jax.named_scope("keys_out"):
        kv = jnp.concatenate([split_heads(key_states), split_heads(value_states)], axis=2)
        kv = lax.all_to_all(kv, TEAM, 0, 0, tiled=True).reshape(512, 2 * DH)
    with jax.named_scope("rows_out"):
        rows = jnp.concatenate([split_heads(queries), split_heads(out_grads)], axis=2)
        rows = lax.all_to_all(rows, TEAM, 0, 0, tiled=True).reshape(512, 2 * GROUP * DH)
    with jax.named_scope("neighbour_keys"):
        kv_prev = lax.ppermute(kv[STRETCH:], CHAIN, forward)
        kv_extra = lax.ppermute(kv, CHAIN, extra)
    spot = jnp.stack(
        [lax.axis_index("xh"), lax.axis_index("yl") * 16 + lax.axis_index("z")]
    ).astype(jnp.int32)
    seg = segment_ids.reshape(2 * PAIRS, STRETCH)
    dq, down, dprev, dextra = attend(spot, rows, kv, kv_prev, kv_extra, seg)
    with jax.named_scope("neighbour_grads"):
        from_next = lax.ppermute(dprev, CHAIN, back(forward)).astype(jnp.float32)
        from_extra = lax.ppermute(dextra, CHAIN, back(extra)).astype(jnp.float32)
        total = down + from_extra + jnp.pad(from_next, ((STRETCH, 0), (0, 0)))
        total = total.astype(jnp.bfloat16).reshape(HK, ROWS, 2 * DH)
    with jax.named_scope("grads_back"):
        sent = jnp.concatenate([dq.reshape(HK, ROWS, GROUP * DH), total], axis=2)
        got = lax.all_to_all(sent, TEAM, 0, 0, tiled=True)
        got = jnp.swapaxes(got, 0, 1).astype(jnp.float32)
        query_grads = got[:, :, : GROUP * DH].reshape(ROWS, HQ * DH)
        key_grads = got[:, :, GROUP * DH : GROUP * DH + DH].reshape(ROWS, HK * DH)
        value_grads = got[:, :, GROUP * DH + DH :].reshape(ROWS, HK * DH)
    return query_grads, key_grads, value_grads


def solution(mesh):
    cut = Mesh(
        mesh.devices.reshape(2, 2, 2, 2, 16, 2), ("xh", "xl", "yh", "yl", "z", "core")
    )
    tokens = P(("yl", "z", "core", "xh", "xl", "yh"), None)
    return jax.shard_map(
        on_device,
        mesh=cut,
        in_specs=(tokens, tokens, tokens, tokens, P()),
        out_specs=(tokens, tokens, tokens),
        check_vma=False,
    )
```

time: 200 us -> 118 us (0.59)
  the two profiles are of different devices: /device:TPU:1 before, /device:TPU:5 now
where the time goes in v1:
time: 118 us
  waiting for transfers between devices  37.1 us (31%)
  starting transfers between devices  29.3 us (25%)
  blocking collectives  26.5 us (22%)
  Pallas kernels  15 us (13%)
  local copies, waits for them, and re-layouts  6.56 us (6%)
  other arithmetic  2.74 us (2%)
    all_to_all x1, blocking collectives, on_device(): got = lax.all_to_all(sent, TEAM, 0, 0, tiled=True)  26.5 us
    ppermute x1, waiting for transfers between devices, on_device(): kv_prev = lax.ppermute(kv[STRETCH:], CHAIN, forward)  19.2 us
    ppermute x1, starting transfers between devices, on_device(): from_extra = lax.ppermute(dextra, CHAIN, back(extra)).astype(jnp.float32)  15.8 us
    pallas_call x1, Pallas kernels, attend(): pl.pallas_call(attend_kernel, out_shape=(jax.ShapeDtypeStruct((512, GROUP...  15 us
    ppermute x1, waiting for transfers between devices, on_device(): from_next = lax.ppermute(dprev, CHAIN, back(forward)).astype(jnp.float32)  7.67 us
    all_to_all x1, starting transfers between devices, on_device(): kv = lax.all_to_all(kv, TEAM, 0, 0, tiled=True).reshape(512, 2 * DH)  5.78 us
    all_to_all x1, waiting for transfers between devices, on_device(): lax.all_to_all(rows, TEAM, 0, 0, tiled=True).reshape(512, 2 * GROUP * DH)  5.48 us
    all_to_all x1, waiting for transfers between devices, on_device(): kv = lax.all_to_all(kv, TEAM, 0, 0, tiled=True).reshape(512, 2 * DH)  4.8 us
  transfers between devices with their start and end apart: 6, of which 4 were waited for; matrix products, arithmetic and copies ran while one was open for 3% of the time, Pallas kernels for 0%

profile of v1, /device:TPU:5, one launch (start us, length us, event | category | flops | bytes accessed | tf_op | source)
XLA Modules:
  0.0 118.0 jit_solution(4833784003779175966)
XLA Ops:
  0.6 0.0 copy-start
  0.6 0.0 copy-start.1
  0.7 0.9 copy-done
  1.5 1.0 bitcast_bitcast_fusion.2
  2.5 0.7 pad_maximum_fusion.2
  3.2 5.8 %all-to-all-start.1 = ((bf16[8,64,256]{2,1,0:T(8,128)(2,1)}), bf16[8,64,256]{2,1,0:T(8,128)(2,1)S(1)}, u32[]{:S(2)}, u32[]{:S(2)}) async-start(bf16[8,64,256]{2,1,0:T(8,128)(2,1)} %pad_maximum_fusion.2), calls=%async_computation.1 | async-start | bytes 524288 | tf_op jit(solution)/shard_map/keys_out/all_to_all | solution.py:188
  9.0 0.0 copy-done.1
  9.0 1.4 %bitcast_bitcast_fusion = (bf16[8,64,1024]{2,1,0:T(8,128)(2,1)S(1)}, bf16[8,64,1024]{2,1,0:T(8,128)(2,1)S(1)}) fusion(bf16[8,8,8,1024]{3,2,1,0:T(8,128)(2,1)S(1)} %bitcast.52, bf16[8,8,8,1024]{3,2,1,0:T(8,128)(2,1)} %bitcast.53), kind=kLoop, calls=%fused_computation.4 | loop fusion | bytes 4194304 | tf_op jit(solution)/shard_map/rows_out/transpose | solution.py:184
  10.5 1.5 %pad_maximum_fusion = bf16[8,64,2048]{2,1,0:T(8,128)(2,1)} fusion(bf16[8,64,1024]{2,1,0:T(8,128)(2,1)S(1)} %get-tuple-element.13, bf16[8,64,1024]{2,1,0:T(8,128)(2,1)S(1)} %get-tuple-element.14), kind=kLoop, calls=%fused_computation.2 | loop fusion | flops 4194304 | bytes 4194304 | tf_op jit(solution)/shard_map/rows_out/concatenate | solution.py:190
  12.0 0.0 copy-start.2
  12.0 4.8 %all-to-all-done.1 = bf16[8,64,256]{2,1,0:T(8,128)(2,1)S(1)} async-done(((bf16[8,64,256]{2,1,0:T(8,128)(2,1)}), bf16[8,64,256]{2,1,0:T(8,128)(2,1)S(1)}, u32[]{:S(2)}, u32[]{:S(2)}) %all-to-all-start.1) | async-done | bytes 262176 | tf_op jit(solution)/shard_map/keys_out/all_to_all | solution.py:188
  16.8 3.9 %all-to-all-start = ((bf16[8,64,2048]{2,1,0:T(8,128)(2,1)}), bf16[8,64,2048]{2,1,0:T(8,128)(2,1)S(1)}, u32[]{:S(2)}, u32[]{:S(2)}) async-start(bf16[8,64,2048]{2,1,0:T(8,128)(2,1)} %pad_maximum_fusion), calls=%async_computation | async-start | bytes 4194304 | tf_op jit(solution)/shard_map/rows_out/all_to_all | solution.py:191
  20.6 1.3 %collective-permute-start.1 = (bf16[512,256]{1,0:T(8,128)(2,1)S(1)}, bf16[512,256]{1,0:T(8,128)(2,1)S(1)}, u32[]{:S(2)}, u32[]{:S(2)}) collective-permute-start(bf16[512,256]{1,0:T(8,128)(2,1)S(1)} %bitcast.48), channel_id=1, source_target_pairs={{62,318},{318,256},{63,319},{319,257},{126,382},{382,320},{127,383... | collective-permute-start | bytes 786440 | tf_op jit(solution)/shard_map/neighbour_keys/ppermute | solution.py:194
  21.9 1.3 %collective-permute-start = (bf16[256,256]{1,0:T(8,128)(2,1)S(1)}, bf16[256,256]{1,0:T(8,128)(2,1)S(1)}, u32[]{:S(2)}, u32[]{:S(2)}) collective-permute-start(bf16[256,256]{1,0:T(8,128)(2,1)S(1)} %bitcast.56), channel_id=1, source_target_pairs={{0,2},{2,4},{4,6},{6,8},{8,10},{10,12},{12,14},{14,16},{16,18},{18... | collective-permute-start | bytes 393224 | tf_op jit(solution)/shard_map/neighbour_keys/ppermute | solution.py:193
  23.3 0.0 copy-done.2
  23.3 0.1 pad_add_fusion.spot_ref
  23.4 19.2 %collective-permute-done.prev_ref = bf16[256,256]{1,0:T(8,128)(2,1)S(1)} collective-permute-done((bf16[256,256]{1,0:T(8,128)(2,1)S(1)}, bf16[256,256]{1,0:T(8,128)(2,1)S(1)}, u32[]{:S(2)}, u32[]{:S(2)}) %collective-permute-start) | collective-permute-done | bytes 131104 | tf_op jit(solution)/shard_map/neighbour_keys/ppermute | solution.py:193
  42.6 0.0 collective-permute-done.1.extra_ref
  42.6 5.5 %all-to-all-done = bf16[8,64,2048]{2,1,0:T(8,128)(2,1)S(1)} async-done(((bf16[8,64,2048]{2,1,0:T(8,128)(2,1)}), bf16[8,64,2048]{2,1,0:T(8,128)(2,1)S(1)}, u32[]{:S(2)}, u32[]{:S(2)}) %all-to-all-start) | async-done | bytes 2097184 | tf_op jit(solution)/shard_map/rows_out/all_to_all | solution.py:191
  48.1 15.0 %attend.1 = (bf16[512,1024]{1,0:T(8,128)(2,1)S(1)}, f32[512,256]{1,0:T(8,128)S(1)}, bf16[256,256]{1,0:T(8,128)(2,1)S(1)}, bf16[512,256]{1,0:T(8,128)(2,1)S(1)}) custom-call(s32[2]{0:T(128)S(1)} %pad_add_fusion.spot_ref, bf16[512,2048]{1,0:T(8,128)(2,1)S(1)} %bitcast.46, bf16[512,256]{1,0:T(8,128)(2,1)S(1)} %bitcast.49, ...), custom_call_target="tpu_custom_call" | custom-call | flops 2684354560 | bytes 6291456 | tf_op jit(solution)/shard_map/attend/pallas_call | solution.py:155
  63.1 15.8 %collective-permute-start.2 = (bf16[512,256]{1,0:T(8,128)(2,1)S(1)}, bf16[512,256]{1,0:T(8,128)(2,1)S(1)}, u32[]{:S(2)}, u32[]{:S(2)}) collective-permute-start(bf16[512,256]{1,0:T(8,128)(2,1)S(1)} %get-tuple-element.9), channel_id=1, source_target_pairs={{318,62},{256,318},{319,63},{257,319},{382,126},{320,382},{383,127... | collective-permute-start | bytes 786440 | tf_op jit(solution)/shard_map/neighbour_grads/ppermute | solution.py:202
  78.9 1.3 %collective-permute-start.3 = (bf16[256,256]{1,0:T(8,128)(2,1)S(1)}, bf16[256,256]{1,0:T(8,128)(2,1)S(1)}, u32[]{:S(2)}, u32[]{:S(2)}) collective-permute-start(bf16[256,256]{1,0:T(8,128)(2,1)S(1)} %get-tuple-element.10), channel_id=1, source_target_pairs={{2,0},{4,2},{6,4},{8,6},{10,8},{12,10},{14,12},{16,14},{18,16},{20... | collective-permute-start | bytes 393224 | tf_op jit(solution)/shard_map/neighbour_grads/ppermute | solution.py:201
  80.2 7.7 %collective-permute-done.3 = bf16[256,256]{1,0:T(8,128)(2,1)S(1)} collective-permute-done((bf16[256,256]{1,0:T(8,128)(2,1)S(1)}, bf16[256,256]{1,0:T(8,128)(2,1)S(1)}, u32[]{:S(2)}, u32[]{:S(2)}) %collective-permute-start.3) | collective-permute-done | bytes 131104 | tf_op jit(solution)/shard_map/neighbour_grads/ppermute | solution.py:201
  87.8 0.0 collective-permute-done.2
  87.8 0.1 add_convert_fusion
  87.9 0.1 pad_maximum_fusion.1
  88.1 26.5 %all_to_all.15 = bf16[8,64,1280]{2,1,0:T(8,128)(2,1)S(1)} all-to-all(bf16[8,64,1280]{2,1,0:T(8,128)(2,1)S(1)} %pad_maximum_fusion.1), channel_id=1, replica_groups=mesh['xh'=2,'xl'=2,'yh'=2,'yl'=2,'z'=16,'core'=2] {'core','xl','yh'}, dimensions={0} | all-to-all | bytes 2621440 | tf_op jit(solution)/shard_map/grads_back/all_to_all | solution.py:207
  114.6 0.2 convert_bitcast_fusion
  114.9 0.3 slice_bitcast_fusion
  115.1 1.5 %copy.19 = f32[8,8,8,1024]{3,2,0,1:T(8,128)} copy(f32[8,8,8,1024]{3,2,1,0:T(8,128)S(1)} %slice_bitcast_fusion) | data formatting | bytes 4194304 | tf_op jit(solution)/shard_map/grads_back/reshape | solution.py:209
  116.6 0.7 copy.28
  117.3 0.7 copy.29
  (3 shorter events, 0.1 us)
Async XLA Ops:
  0.6 0.9 copy-start
  0.6 8.4 %copy-start.1 = (bf16[64,8192]{1,0:T(8,128)(2,1)S(1)}, bf16[64,8192]{1,0:T(8,128)(2,1)}, u32[]{:S(2)}) copy-start(bf16[64,8192]{1,0:T(8,128)(2,1)} %param.8) | copy-start | bytes 3145732
  3.2 13.5 %all-to-all-start.1 = ((bf16[8,64,256]{2,1,0:T(8,128)(2,1)}), bf16[8,64,256]{2,1,0:T(8,128)(2,1)S(1)}, u32[]{:S(2)}, u32[]{:S(2)}) async-start(bf16[8,64,256]{2,1,0:T(8,128)(2,1)} %pad_maximum_fusion.2), calls=%async_computation.1 | async-start | bytes 524288 | tf_op jit(solution)/shard_map/keys_out/all_to_all | solution.py:188
  12.0 11.3 %copy-start.2 = (s32[32768]{0:T(1024)S(1)}, s32[32768]{0:T(1024)}, u32[]{:S(2)}) copy-start(s32[32768]{0:T(1024)} %param.9) | copy-start | bytes 393220
  16.8 31.3 %all-to-all-start = ((bf16[8,64,2048]{2,1,0:T(8,128)(2,1)}), bf16[8,64,2048]{2,1,0:T(8,128)(2,1)S(1)}, u32[]{:S(2)}, u32[]{:S(2)}) async-start(bf16[8,64,2048]{2,1,0:T(8,128)(2,1)} %pad_maximum_fusion), calls=%async_computation | async-start | bytes 4194304 | tf_op jit(solution)/shard_map/rows_out/all_to_all | solution.py:191
  20.6 21.9 %collective-permute-start.1 = (bf16[512,256]{1,0:T(8,128)(2,1)S(1)}, bf16[512,256]{1,0:T(8,128)(2,1)S(1)}, u32[]{:S(2)}, u32[]{:S(2)}) collective-permute-start(bf16[512,256]{1,0:T(8,128)(2,1)S(1)} %bitcast.48), channel_id=1, source_target_pairs={{62,318},{318,256},{63,319},{319,257},{126,382},{382,320},{127,383... | collective-permute-start | bytes 786440 | tf_op jit(solution)/shard_map/neighbour_keys/ppermute | solution.py:194
  21.9 20.6 %collective-permute-start = (bf16[256,256]{1,0:T(8,128)(2,1)S(1)}, bf16[256,256]{1,0:T(8,128)(2,1)S(1)}, u32[]{:S(2)}, u32[]{:S(2)}) collective-permute-start(bf16[256,256]{1,0:T(8,128)(2,1)S(1)} %bitcast.56), channel_id=1, source_target_pairs={{0,2},{2,4},{4,6},{6,8},{8,10},{10,12},{12,14},{14,16},{16,18},{18... | collective-permute-start | bytes 393224 | tf_op jit(solution)/shard_map/neighbour_keys/ppermute | solution.py:193
  63.1 24.7 %collective-permute-start.2 = (bf16[512,256]{1,0:T(8,128)(2,1)S(1)}, bf16[512,256]{1,0:T(8,128)(2,1)S(1)}, u32[]{:S(2)}, u32[]{:S(2)}) collective-permute-start(bf16[512,256]{1,0:T(8,128)(2,1)S(1)} %get-tuple-element.9), channel_id=1, source_target_pairs={{318,62},{256,318},{319,63},{257,319},{382,126},{320,382},{383,127... | collective-permute-start | bytes 786440 | tf_op jit(solution)/shard_map/neighbour_grads/ppermute | solution.py:202
  78.9 9.0 %collective-permute-start.3 = (bf16[256,256]{1,0:T(8,128)(2,1)S(1)}, bf16[256,256]{1,0:T(8,128)(2,1)S(1)}, u32[]{:S(2)}, u32[]{:S(2)}) collective-permute-start(bf16[256,256]{1,0:T(8,128)(2,1)S(1)} %get-tuple-element.10), channel_id=1, source_target_pairs={{2,0},{4,2},{6,4},{8,6},{10,8},{12,10},{14,12},{16,14},{18,16},{20... | collective-permute-start | bytes 393224 | tf_op jit(solution)/shard_map/neighbour_grads/ppermute | solution.py:201

commit v2 on v1

v2 whole, which is shorter than its diff:
```python
import math

import jax
import jax.numpy as jnp
from jax import lax
from jax.experimental import pallas as pl
from jax.experimental.pallas import tpu as pltpu
from jax.sharding import Mesh, PartitionSpec as P

HQ = 64
HK = 8
DH = 128
STRETCH = 256
GROUP = HQ // HK
PAIRS = 64
ROWS = 64
WIDE = GROUP * DH
LAST = PAIRS // 2 - 1

FACTOR = 1.0 / math.sqrt(DH)
LOG2E = 1.4426950408889634
FILL = -1e30

TEAM = ("core", "xl", "yh")
CHAIN = ("xh", "xl", "yl", "z")

OWN0, OWN1, NEAR, FAR = (i * STRETCH for i in range(4))


def chain_pairs():
    def at(late, xl, n):
        return (late * 2 + xl) * (PAIRS // 2) + n

    odd, odd_extra, even_extra = [], [], []
    for xl in (0, 1):
        odd += [(at(0, xl, n), at(0, xl, n + 1)) for n in range(LAST)]
        odd += [(at(0, xl, LAST), at(1, 1 - xl, 0))]
        odd_extra += [(at(0, xl, LAST), at(1, 1 - xl, LAST)), (at(1, xl, LAST), at(1, xl, 0))]
        even_extra += [(at(0, xl, LAST), at(1, 1 - xl, LAST))]
    return odd, odd_extra, even_extra


def back(pairs):
    return [(b, a) for a, b in pairs]


def nt_dot(a, b):
    return lax.dot_general(a, b, (((1,), (1,)), ((), ())), preferred_element_type=jnp.float32)


def nn_dot(a, b):
    return lax.dot_general(a, b, (((1,), (0,)), ((), ())), preferred_element_type=jnp.float32)


def x_head(label, core):
    return label * 2 + core


def y_head(yh, core):
    return HK // 2 + yh * 2 + core


def span(start, size):
    return pl.ds(pl.multiple_of(start, size), size)


def labels():
    late, xl, yh, core = (lax.axis_index(name) for name in ("xh", "xl", "yh", "core"))
    n = lax.axis_index("yl") * 16 + lax.axis_index("z")
    return late, n, xl, yh, core, jnp.where(late == 1, 1 - xl, xl)


def kinds(core):
    _, _, _, yh, _, lab = labels()
    return x_head(lab, core), x_head(1 - lab, core), y_head(yh, core), y_head(1 - yh, core)


def pack_kernel(k_ref, v_ref, q_ref, g_ref, kv_ref, keep_ref, swap_ref, x_ref, y_ref):
    late = lax.axis_index("xh")
    for core in (0, 1):
        for xl in (0, 1):
            for yh in (0, 1):
                d = core * 4 + xl * 2 + yh
                hx = x_head(jnp.where(late == 1, 1 - xl, xl), core)
                hy = y_head(yh, core)
                kv_ref[d, :, 0:DH] = k_ref[:, span(hx * DH, DH)]
                kv_ref[d, :, DH : 2 * DH] = v_ref[:, span(hx * DH, DH)]
                kv_ref[d, :, 2 * DH : 3 * DH] = k_ref[:, hy * DH : hy * DH + DH]
                kv_ref[d, :, 3 * DH : 4 * DH] = v_ref[:, hy * DH : hy * DH + DH]
    core = lax.axis_index("core")
    near = (keep_ref.at[0], x_ref, keep_ref.at[1], y_ref)
    for bit, outs in ((1 - core, [swap_ref.at[i] for i in range(4)]), (core, near)):
        for out, head in zip(outs, kinds(bit)):
            out[:, 0:WIDE] = q_ref[:, span(head * WIDE, WIDE)]
            out[:, WIDE : 2 * WIDE] = g_ref[:, span(head * WIDE, WIDE)]


def attend_kernel(
    x_ref, y_ref, keep_ref, got_ref, own_ref, prev_ref, odd_ref, even_ref, seg_ref,
    dq_near, dq_swap, dq_x, dq_y, down_ref, dnear_ref, dfar_ref,
    rows, dq, kv, kt, acc, bias, arrived,
):
    late, n, xl, yh, core, _ = labels()
    early = late == 0
    first = (late == 1) & (n == 0)
    final = (late == 1) & (n == LAST)

    pieces = []
    for i, pair in ((0, core), (1, 1 - core)):
        pieces.append((x_ref.at[i], rows.at[0, pair, 1 - xl]))
        pieces.append((y_ref.at[i], rows.at[1, pair, 1 - yh]))
    copies = [pltpu.make_async_copy(a, b, arrived.at[i]) for i, (a, b) in enumerate(pieces)]
    for copy in copies:
        copy.start()
    rows[0, core, xl] = keep_ref[0]
    rows[0, 1 - core, xl] = got_ref[0]
    rows[1, core, yh] = keep_ref[1]
    rows[1, 1 - core, yh] = got_ref[2]

    def stage(at, ref, row):
        for part in (0, 1):
            block = ref[row : row + STRETCH, part * 2 * DH : (part + 1) * 2 * DH]
            kv[part, at : at + STRETCH, :] = block
            kt[part, :, at : at + STRETCH] = block[:, 0:DH].T
            acc[part, at : at + STRETCH, :] = jnp.zeros((STRETCH, 2 * DH), jnp.float32)

    stage(OWN0, own_ref, 0)
    stage(OWN1, own_ref, STRETCH)

    @pl.when(early | first)
    def _():
        stage(NEAR, prev_ref, 0)

    @pl.when(final)
    def _():
        stage(NEAR, even_ref, 0)

    @pl.when(first | final)
    def _():
        stage(FAR, odd_ref, 0)

    for copy in copies:
        copy.wait()

    def doc_row(block):
        return jnp.concatenate(
            [seg_ref[pl.ds(2 * block, 1), :], seg_ref[pl.ds(2 * block + 1, 1), :]], axis=1
        )

    def fill_bias(place, part, q_block, k_block):
        docs = doc_row(q_block)
        even = jnp.concatenate([docs[:, 0:64], docs[:, 128:192]], axis=1)
        odd = jnp.concatenate([docs[:, 64:128], docs[:, 192:256]], axis=1)
        x_doc = jnp.where(yh == 0, even, odd)
        y_doc = jnp.where(xl == 0, docs[:, :DH], docs[:, DH:])
        q_doc = jnp.where(part == 0, x_doc, y_doc).astype(jnp.float32)
        k_doc = jnp.broadcast_to(doc_row(k_block), (DH, STRETCH))
        k_doc = k_doc.astype(jnp.float32).T
        lane = lax.broadcasted_iota(jnp.int32, (STRETCH, DH), 1)
        x_row = lane + jnp.where(lane >= ROWS, ROWS, 0) + yh * ROWS
        q_pos = q_block * STRETCH + jnp.where(part == 0, x_row, lane + xl * DH)
        k_pos = k_block * STRETCH + lax.broadcasted_iota(jnp.int32, (STRETCH, DH), 0)
        ok = (k_pos <= q_pos) & (k_doc == q_doc)
        bias[place] = jnp.where(ok, 0.0, FILL)

    def unit(part, pair, offsets):
        def stack(base, h0):
            return jnp.concatenate(
                [
                    rows[part, pair, s, :, base + h * DH : base + (h + 1) * DH]
                    for h in range(h0, h0 + 2)
                    for s in (0, 1)
                ],
                axis=0,
            )

        def products(h0):
            q, g = stack(0, h0), stack(WIDE, h0)
            scores = [nt_dot(kv[part, pl.ds(o, STRETCH), 0:DH], q) for o in offsets]
            wgrads = [nt_dot(kv[part, pl.ds(o, STRETCH), DH : 2 * DH], g) for o in offsets]
            return q, g, scores, wgrads

        def softmax(scores, wgrads):
            scores = [
                s * (FACTOR * LOG2E) + jnp.concatenate([bias[i]] * 2, axis=1)
                for i, s in enumerate(scores)
            ]
            peak = jnp.max(scores[0], axis=0, keepdims=True)
            for s in scores[1:]:
                peak = jnp.maximum(peak, jnp.max(s, axis=0, keepdims=True))
            exps = [jnp.exp2(s - peak) for s in scores]
            total = sum(jnp.sum(e, axis=0, keepdims=True) for e in exps)
            delta = sum(jnp.sum(e * w, axis=0, keepdims=True) for e, w in zip(exps, wgrads))
            inverse = 1.0 / total
            delta = delta * inverse
            weights = [e * inverse for e in exps]
            grads = [(p * (w - delta)).astype(jnp.bfloat16) for p, w in zip(weights, wgrads)]
            return [p.astype(jnp.bfloat16) for p in weights], grads

        def spread(h0, q, g, weights, grads):
            dq_t = sum(nn_dot(kt[part, :, pl.ds(o, STRETCH)], d) for o, d in zip(offsets, grads))
            dq_rows = (dq_t * FACTOR).T.astype(jnp.bfloat16)
            for h in range(2):
                for s in (0, 1):
                    at = (2 * h + s) * ROWS
                    dq[part, pair, s, :, (h0 + h) * DH : (h0 + h + 1) * DH] = dq_rows[at : at + ROWS]
            return [nn_dot(d, q) for d in grads], [nn_dot(p, g) for p in weights]

        outs = []
        ahead = products(0)
        for step in range(4):
            this = ahead
            if step < 3:
                ahead = products(2 * step + 2)
            outs.append(spread(2 * step, *this[:2], *softmax(*this[2:])))

        for i, o in enumerate(offsets):
            acc[part, pl.ds(o, STRETCH), 0:DH] += sum(k[i] for k, _ in outs)
            acc[part, pl.ds(o, STRETCH), DH : 2 * DH] += sum(v[i] for _, v in outs)

    def run(pair, q_block, offsets, blocks):
        @pl.loop(0, 2)
        def _(part):
            for i in range(len(offsets)):
                fill_bias(i, part, q_block, blocks[i])
            unit(part, pair, offsets)

    def block_of(pair):
        return jnp.where(early, pair, 2 * PAIRS - 1 - pair)

    b0 = block_of(2 * n)
    b1 = block_of(2 * n + 1)
    end_early = PAIRS - 1
    end_late = PAIRS

    @pl.when((early & (n == 0)) | ((late == 1) & (n != 0) & (n != LAST)))
    def _():
        run(0, b0, [OWN0], [b0])

    @pl.when((early & (n > 0)) | final)
    def _():
        run(0, b0, [OWN0, NEAR], [b0, jnp.where(early, 2 * n - 1, end_early - 1)])

    @pl.when(first)
    def _():
        run(0, b0, [OWN0, NEAR, FAR], [b0, end_early, end_late])

    @pl.when((late == 1) & (n != LAST))
    def _():
        run(1, b1, [OWN1], [b1])

    @pl.when(early)
    def _():
        run(1, b1, [OWN1, OWN0], [b1, b0])

    @pl.when(final)
    def _():
        run(1, b1, [OWN1, NEAR, FAR], [b1, end_early - 1, end_early])

    dq_near[0] = dq[0, core, xl]
    dq_near[1] = dq[1, core, yh]
    dq_x[...] = dq[0, core, 1 - xl]
    dq_y[...] = dq[1, core, 1 - yh]
    dq_swap[0] = dq[0, 1 - core, xl]
    dq_swap[1] = dq[0, 1 - core, 1 - xl]
    dq_swap[2] = dq[1, 1 - core, yh]
    dq_swap[3] = dq[1, 1 - core, 1 - yh]

    def give(out, at, size):
        for part in (0, 1):
            k_cols = slice(part * 2 * DH, part * 2 * DH + DH)
            v_cols = slice(part * 2 * DH + DH, (part + 1) * 2 * DH)
            out[:, k_cols] = (acc[part, at : at + size, 0:DH] * FACTOR).astype(out.dtype)
            out[:, v_cols] = acc[part, at : at + size, DH : 2 * DH].astype(out.dtype)

    give(down_ref, OWN0, 512)

    @pl.when(early | first | final)
    def _():
        give(dnear_ref, NEAR, 256)

    @pl.when(first | final)
    def _():
        give(dfar_ref, FAR, 256)


def unpack_rows_kernel(dq_near, got_ref, x_ref, y_ref, q_out):
    _, _, _, yh, core, lab = labels()

    def put(head, block):
        q_out[:, span(head * WIDE, WIDE)] = block.astype(jnp.float32)

    put(x_head(lab, core), dq_near[0])
    put(x_head(lab, 1 - core), got_ref[0])
    put(y_head(yh, core), dq_near[1])
    put(y_head(yh, 1 - core), got_ref[2])
    for i, bit in ((0, core), (1, 1 - core)):
        put(x_head(1 - lab, bit), x_ref[i])
        put(y_head(1 - yh, bit), y_ref[i])


def unpack_keys_kernel(kv_ref, k_out, v_out):
    late = lax.axis_index("xh")

    def term(c, x, y, at):
        return kv_ref[c * 4 + x * 2 + y, :, at * DH : (at + 1) * DH].astype(jnp.float32)

    for c in (0, 1):
        for b in (0, 1):
            hx = x_head(jnp.where(late == 1, 1 - b, b), c)
            k_out[:, span(hx * DH, DH)] = term(c, b, 0, 0) + term(c, b, 1, 0)
            v_out[:, span(hx * DH, DH)] = term(c, b, 0, 1) + term(c, b, 1, 1)
            hy = y_head(b, c)
            k_out[:, hy * DH : hy * DH + DH] = term(c, 0, b, 2) + term(c, 1, b, 2)
            v_out[:, hy * DH : hy * DH + DH] = term(c, 0, b, 3) + term(c, 1, b, 3)


def call(kernel, name, inputs, outputs, scratch=(), limit=32, moved=1024, outside=0):
    vmem = pl.BlockSpec(memory_space=pltpu.VMEM)
    return pl.pallas_call(
        kernel,
        out_shape=tuple(jax.ShapeDtypeStruct(s, d) for s, d in outputs),
        in_specs=[pl.BlockSpec(memory_space=pl.ANY)] * outside + [vmem] * (len(inputs) - outside),
        out_specs=(vmem,) * len(outputs),
        scratch_shapes=list(scratch),
        compiler_params=pltpu.CompilerParams(vmem_limit_bytes=limit * 2**20),
        cost_estimate=pl.CostEstimate(flops=0, bytes_accessed=moved, transcendentals=0),
        name=name,
    )(*inputs)


def on_device(queries, key_states, value_states, out_grads, segment_ids):
    odd, odd_extra, even_extra = chain_pairs()
    low, wide = jnp.bfloat16, jnp.float32

    def swap(array, axis):
        return lax.ppermute(array, axis, [(0, 1), (1, 0)])

    four = ((4, ROWS, 2 * WIDE), low)
    two = ((2, ROWS, 2 * WIDE), low)
    one = ((ROWS, 2 * WIDE), low)
    kv, keep, sent, x_rows, y_rows = call(
        pack_kernel, "pack", (key_states, value_states, queries, out_grads),
        [((8, ROWS, 4 * DH), low), two, four, one, one], limit=60,
    )
    kv = lax.all_to_all(kv, TEAM, 0, 0, tiled=True).reshape(512, 4 * DH)
    got = swap(sent, "core")
    x_rows = jnp.stack([x_rows, got[1]])
    y_rows = jnp.stack([y_rows, got[3]])
    x_rows = swap(x_rows, "xl")
    y_rows = swap(y_rows, "yh")
    kv_prev = lax.ppermute(kv[STRETCH:], CHAIN, odd)
    kv_odd = lax.ppermute(kv[STRETCH:], CHAIN, odd_extra)
    kv_even = lax.ppermute(kv[:STRETCH], CHAIN, even_extra)
    seg = segment_ids.reshape(4 * PAIRS, DH)

    one = ((ROWS, WIDE), low)
    two = ((2, ROWS, WIDE), low)
    four = ((4, ROWS, WIDE), low)
    dq_near, sent, dq_x, dq_y, down, dnear, dfar = call(
        attend_kernel, "attend",
        (x_rows, y_rows, keep, got, kv, kv_prev, kv_odd, kv_even, seg),
        [two, four, one, one, ((512, 4 * DH), wide)] + [((256, 4 * DH), low)] * 2,
        scratch=[
            pltpu.VMEM((2, 2, 2, ROWS, 2 * WIDE), low),
            pltpu.VMEM((2, 2, 2, ROWS, WIDE), low),
            pltpu.VMEM((2, 4 * STRETCH, 2 * DH), low),
            pltpu.VMEM((2, DH, 4 * STRETCH), low),
            pltpu.VMEM((2, 4 * STRETCH, 2 * DH), wide),
            pltpu.VMEM((3, STRETCH, DH), wide),
            pltpu.SemaphoreType.DMA((4,)),
        ],
        limit=40, outside=2,
    )
    from_next = lax.ppermute(dnear, CHAIN, back(odd))
    from_even = lax.ppermute(dnear, CHAIN, back(even_extra))
    from_odd = lax.ppermute(dfar, CHAIN, back(odd_extra))
    got = swap(sent, "core")
    dq_x = jnp.stack([dq_x, got[1]])
    dq_y = jnp.stack([dq_y, got[3]])
    dq_x = swap(dq_x, "xl")
    dq_y = swap(dq_y, "yh")
    dq_x, dq_y, from_next, from_even, from_odd = lax.optimization_barrier(
        (dq_x, dq_y, from_next, from_even, from_odd)
    )
    add = jnp.concatenate(
        [from_even.astype(wide), from_next.astype(wide) + from_odd.astype(wide)], axis=0
    )
    total = (down + add).astype(low).reshape(HK, ROWS, 4 * DH)
    total = lax.all_to_all(total, TEAM, 0, 0, tiled=True)
    (query_grads,) = call(
        unpack_rows_kernel, "unpack_rows", (dq_near, got, dq_x, dq_y),
        [((ROWS, HQ * DH), wide)], moved=32 * 2**20,
    )
    query_grads, total = lax.optimization_barrier((query_grads, total))
    key_grads, value_grads = call(
        unpack_keys_kernel, "unpack_keys", (total,), [((ROWS, HK * DH), wide)] * 2
    )
    return query_grads, key_grads, value_grads


def solution(mesh):
    cut = Mesh(
        mesh.devices.reshape(2, 2, 2, 2, 16, 2), ("xh", "xl", "yh", "yl", "z", "core")
    )
    tokens = P(("yl", "z", "core", "xh", "xl", "yh"), None)
    return jax.shard_map(
        on_device,
        mesh=cut,
        in_specs=(tokens, tokens, tokens, tokens, P()),
        out_specs=(tokens, tokens, tokens),
        check_vma=False,
    )
```

time: 118 us -> 96.8 us (0.82)
  blocking collectives: 26.5 us -> 0 us
  starting transfers between devices: 29.3 us -> 38 us
  local copies, waits for them, and re-layouts: 6.56 us -> 0.11 us
  waiting for transfers between devices: 37.1 us -> 39.5 us
    all_to_all x1 -> x0, blocking collectives: 26.5 us -> none  [on_device(): got = lax.all_to_all(sent, TEAM, 0, 0, tiled=True)]
    ppermute x4 -> x12, starting transfers between devices: 19.6 us -> 27.9 us  [the longest x6 18.9 us: swap(): return lax.ppermute(array, axis, [(0, 1), (1, 0)])]
    reshape x4 -> x0, local copies, waits for them, and re-layouts: 2.94 us -> none  [the longest x1 1.46 us: on_device(): query_grads = got[:, :, :GROUP * DH].reshape(ROWS, HQ * DH)]
    transpose x2 -> x0, local copies, waits for them, and re-layouts: 2.39 us -> none  [split_heads(): return jnp.swapaxes(array.reshape(ROWS, HK, -1), 0, 1)]
    concatenate x3 -> x0, other arithmetic: 2.34 us -> none  [the longest x1 1.51 us: on_device(): jnp.concatenate([split_heads(queries), split_heads(out_grads)], axis=2)]
    ppermute x4 -> x12, waiting for transfers between devices: 26.9 us -> 29 us  [the longest x1 17.8 us: on_device(): kv_odd = lax.ppermute(kv[STRETCH:], CHAIN, odd_extra)]
    another operation x1 -> x4, other arithmetic: 0.08 us -> 1.75 us  [the longest x1 0.85 us: on_device(): y_rows = jnp.stack([y_rows, got[3]])]
    unnamed x8, local copies, waits for them, and re-layouts: 1.21 us -> 0.01 us
  transfers between devices with their start and end apart: 6 -> 14, of which waited for: 4 -> 7; matrix products, arithmetic and copies ran while one was open for 3% -> 2% of each run, Pallas kernels for 0% -> 2%
where the time goes in v2:
time: 96.8 us; the launch traced here: 96.2 us
  waiting for transfers between devices  39.5 us (41%)
  starting transfers between devices  38 us (39%)
  Pallas kernels  15 us (15%)
  other arithmetic  2.83 us (3%)
    ppermute x6, starting transfers between devices, swap(): return lax.ppermute(array, axis, [(0, 1), (1, 0)])  18.9 us
    ppermute x1, waiting for transfers between devices, on_device(): kv_odd = lax.ppermute(kv[STRETCH:], CHAIN, odd_extra)  17.8 us
    pallas_call x4, Pallas kernels, call(): pl.pallas_call(kernel, out_shape=tuple((jax.ShapeDtypeStruct(s, d) for s,...  15 us
    all_to_all x1, waiting for transfers between devices, on_device(): total = lax.all_to_all(total, TEAM, 0, 0, tiled=True)  9.09 us
    ppermute x6, waiting for transfers between devices, swap(): return lax.ppermute(array, axis, [(0, 1), (1, 0)])  5.78 us
    all_to_all x1, starting transfers between devices, on_device(): kv = lax.all_to_all(kv, TEAM, 0, 0, tiled=True).reshape(512, 4 * DH)  5.23 us
    all_to_all x1, starting transfers between devices, on_device(): total = lax.all_to_all(total, TEAM, 0, 0, tiled=True)  4.85 us
    ppermute x1, waiting for transfers between devices, on_device(): kv_prev = lax.ppermute(kv[STRETCH:], CHAIN, odd)  3.54 us
  transfers between devices with their start and end apart: 14, of which 7 were waited for; matrix products, arithmetic and copies ran while one was open for 2% of the time, Pallas kernels for 2%

profile of v2, /device:TPU:5, one launch (start us, length us, event | category | flops | bytes accessed | tf_op | source)
XLA Modules:
  0.0 96.2 jit_solution(639058778872922729)
XLA Ops:
  0.6 3.4 %pack.1 = (bf16[8,64,512]{2,1,0:T(8,128)(2,1)}, bf16[2,64,2048]{2,1,0:T(8,128)(2,1)}, bf16[4,64,2048]{2,1,0:T(8,128)(2,1)}, bf16[64,2048]{1,0:T(8,128)(2,1)}, bf16[64,2048]{1,0:T(8,128)(2,1)}) custom-call(bf16[64,1024]{1,0:T(8,128)(2,1)} %k_ref.1, bf16[64,1024]{1,0:T(8,128)(2,1)} %v_ref.1, bf16[64,8192]{1,0:T(8,128)(2,1)} %q_ref.1, bf16[64,8192]{1,0:T(8,128)(2,1)} %g_ref.1), custom_call_target="tpu_custom_call" | custom-call | bytes 1024 | tf_op jit(solution)/shard_map/pack/pallas_call | solution.py:320
  4.0 0.0 copy-start.3
  4.0 0.0 copy-start.2
  4.0 2.7 %collective-permute-start = (bf16[4,64,2048]{2,1,0:T(8,128)(2,1)}, bf16[4,64,2048]{2,1,0:T(8,128)(2,1)S(1)}, u32[]{:S(2)}, u32[]{:S(2)}) collective-permute-start(bf16[4,64,2048]{2,1,0:T(8,128)(2,1)} %get-tuple-element.25), channel_id=1, source_target_pairs={{0,1},{1,0},{2,3},{3,2},{4,5},{5,4},{6,7},{7,6},{8,9},{9,8},{10,11... | collective-permute-start | bytes 3145736 | tf_op jit(solution)/shard_map/ppermute | solution.py:337
  6.7 5.2 %all-to-all-start = ((bf16[8,64,512]{2,1,0:T(8,128)(2,1)}), bf16[8,64,512]{2,1,0:T(8,128)(2,1)S(1)}, u32[]{:S(2)}, u32[]{:S(2)}) async-start(bf16[8,64,512]{2,1,0:T(8,128)(2,1)} %get-tuple-element.28), calls=%async_computation | async-start | bytes 1048576 | tf_op jit(solution)/shard_map/all_to_all | solution.py:346
  11.9 0.0 copy-start
  11.9 0.0 copy-start.1
  12.0 0.0 collective-permute-done.got_ref
  12.0 0.0 copy-done.3
  12.0 0.8 pad_maximum_fusion
  12.9 3.3 %collective-permute-start.1 = (bf16[2,64,2048]{2,1,0:T(8,128)(2,1)}, bf16[2,64,2048]{2,1,0:T(8,128)(2,1)S(1)}, u32[]{:S(2)}, u32[]{:S(2)}) collective-permute-start(bf16[2,64,2048]{2,1,0:T(8,128)(2,1)} %pad_maximum_fusion), channel_id=1, source_target_pairs={{0,128},{128,0},{1,129},{129,1},{2,130},{130,2},{3,131},{131,3},{4... | collective-permute-start | bytes 1572872 | tf_op jit(solution)/shard_map/ppermute | solution.py:337
  16.1 0.0 copy-done.2
  16.2 0.9 pad_maximum_fusion.1
  17.0 4.6 %collective-permute-start.2 = (bf16[2,64,2048]{2,1,0:T(8,128)(2,1)}, bf16[2,64,2048]{2,1,0:T(8,128)(2,1)S(1)}, u32[]{:S(2)}, u32[]{:S(2)}) collective-permute-start(bf16[2,64,2048]{2,1,0:T(8,128)(2,1)} %pad_maximum_fusion.1), channel_id=1, source_target_pairs={{0,64},{64,0},{1,65},{65,1},{2,66},{66,2},{3,67},{67,3},{4,68},{68... | collective-permute-start | bytes 1572872 | tf_op jit(solution)/shard_map/ppermute | solution.py:337
  21.6 1.4 %all-to-all-done = bf16[8,64,512]{2,1,0:T(8,128)(2,1)S(1)} async-done(((bf16[8,64,512]{2,1,0:T(8,128)(2,1)}), bf16[8,64,512]{2,1,0:T(8,128)(2,1)S(1)}, u32[]{:S(2)}, u32[]{:S(2)}) %all-to-all-start) | async-done | bytes 524320 | tf_op jit(solution)/shard_map/all_to_all | solution.py:346
  23.0 0.7 collective-permute-start.5
  23.7 1.3 %collective-permute-start.4 = (bf16[256,512]{1,0:T(8,128)(2,1)S(1)}, bf16[256,512]{1,0:T(8,128)(2,1)S(1)}, u32[]{:S(2)}, u32[]{:S(2)}) collective-permute-start(bf16[256,512]{1,0:T(8,128)(2,1)S(1)} %bitcast.15), channel_id=1, source_target_pairs={{62,446},{318,256},{190,318},{446,384},{63,447},{319,257},{191,319... | collective-permute-start | bytes 786440 | tf_op jit(solution)/shard_map/ppermute | solution.py:353
  25.0 1.3 %collective-permute-start.3 = (bf16[256,512]{1,0:T(8,128)(2,1)S(1)}, bf16[256,512]{1,0:T(8,128)(2,1)S(1)}, u32[]{:S(2)}, u32[]{:S(2)}) collective-permute-start(bf16[256,512]{1,0:T(8,128)(2,1)S(1)} %bitcast.16), channel_id=1, source_target_pairs={{0,2},{2,4},{4,6},{6,8},{8,10},{10,12},{12,14},{14,16},{16,18},{18... | collective-permute-start | bytes 786440 | tf_op jit(solution)/shard_map/ppermute | solution.py:352
  26.3 0.0 collective-permute-done.5.even_ref
  26.3 17.8 %collective-permute-done.4.odd_ref = bf16[256,512]{1,0:T(8,128)(2,1)S(1)} collective-permute-done((bf16[256,512]{1,0:T(8,128)(2,1)S(1)}, bf16[256,512]{1,0:T(8,128)(2,1)S(1)}, u32[]{:S(2)}, u32[]{:S(2)}) %collective-permute-start.4) | collective-permute-done | bytes 262176 | tf_op jit(solution)/shard_map/ppermute | solution.py:353
  44.1 3.5 %collective-permute-done.3.prev_ref = bf16[256,512]{1,0:T(8,128)(2,1)S(1)} collective-permute-done((bf16[256,512]{1,0:T(8,128)(2,1)S(1)}, bf16[256,512]{1,0:T(8,128)(2,1)S(1)}, u32[]{:S(2)}, u32[]{:S(2)}) %collective-permute-start.3) | collective-permute-done | bytes 262176 | tf_op jit(solution)/shard_map/ppermute | solution.py:352
  47.6 0.0 collective-permute-done.1.x_ref
  47.6 0.0 collective-permute-done.2.y_ref
  47.6 0.0 copy-done
  47.7 0.0 copy-done.1
  47.7 9.3 %attend.1 = (bf16[2,64,1024]{2,1,0:T(8,128)(2,1)S(1)}, bf16[4,64,1024]{2,1,0:T(8,128)(2,1)S(1)}, bf16[64,1024]{1,0:T(8,128)(2,1)S(1)}, bf16[64,1024]{1,0:T(8,128...) custom-call(bf16[2,64,2048]{2,1,0:T(8,128)(2,1)S(1)} %collective-permute-done.1.x_ref, ...), custom_call_target="tpu_custom_call" | custom-call | bytes 1024 | tf_op jit(solution)/shard_map/attend/pallas_call | solution.py:320
  57.0 2.6 %collective-permute-start.6 = (bf16[4,64,1024]{2,1,0:T(8,128)(2,1)S(1)}, bf16[4,64,1024]{2,1,0:T(8,128)(2,1)S(1)}, u32[]{:S(2)}, u32[]{:S(2)}) collective-permute-start(bf16[4,64,1024]{2,1,0:T(8,128)(2,1)S(1)} %get-tuple-element.30), channel_id=1, source_target_pairs={{0,1},{1,0},{2,3},{3,2},{4,5},{5,4},{6,7},{7,6},{8,9},{9,8},{10,11... | collective-permute-start | bytes 1572872 | tf_op jit(solution)/shard_map/ppermute | solution.py:337
  59.6 0.7 collective-permute-start.10
  60.3 1.5 %collective-permute-start.9 = (bf16[256,512]{1,0:T(8,128)(2,1)S(1)}, bf16[256,512]{1,0:T(8,128)(2,1)S(1)}, u32[]{:S(2)}, u32[]{:S(2)}) collective-permute-start(bf16[256,512]{1,0:T(8,128)(2,1)S(1)} %get-tuple-element.33), channel_id=1, source_target_pairs={{2,0},{4,2},{6,4},{8,6},{10,8},{12,10},{14,12},{16,14},{18,16},{20... | collective-permute-start | bytes 786440 | tf_op jit(solution)/shard_map/ppermute | solution.py:375
  61.8 3.5 %collective-permute-start.11 = (bf16[256,512]{1,0:T(8,128)(2,1)S(1)}, bf16[256,512]{1,0:T(8,128)(2,1)S(1)}, u32[]{:S(2)}, u32[]{:S(2)}) collective-permute-start(bf16[256,512]{1,0:T(8,128)(2,1)S(1)} %get-tuple-element.34), channel_id=1, source_target_pairs={{446,62},{256,318},{318,190},{384,446},{447,63},{257,319},{319,191... | collective-permute-start | bytes 786440 | tf_op jit(solution)/shard_map/ppermute | solution.py:377
  65.3 0.0 collective-permute-done.6.got_ref
  65.4 2.7 %collective-permute-start.7 = (bf16[2,64,1024]{2,1,0:T(8,128)(2,1)S(1)}, bf16[2,64,1024]{2,1,0:T(8,128)(2,1)S(1)}, u32[]{:S(2)}, u32[]{:S(2)}) collective-permute-start(bf16[2,64,1024]{2,1,0:T(8,128)(2,1)S(1)} %pad_maximum_fusion.2), channel_id=1, source_target_pairs={{0,128},{128,0},{1,129},{129,1},{2,130},{130,2},{3,131},{131,3},{4... | collective-permute-start | bytes 786440 | tf_op jit(solution)/shard_map/ppermute | solution.py:337
  68.2 3.0 %collective-permute-start.8 = (bf16[2,64,1024]{2,1,0:T(8,128)(2,1)S(1)}, bf16[2,64,1024]{2,1,0:T(8,128)(2,1)S(1)}, u32[]{:S(2)}, u32[]{:S(2)}) collective-permute-start(bf16[2,64,1024]{2,1,0:T(8,128)(2,1)S(1)} %pad_maximum_fusion.3), channel_id=1, source_target_pairs={{0,64},{64,0},{1,65},{65,1},{2,66},{66,2},{3,67},{67,3},{4,68},{68... | collective-permute-start | bytes 786440 | tf_op jit(solution)/shard_map/ppermute | solution.py:337
  71.2 1.9 %collective-permute-done.11 = bf16[256,512]{1,0:T(8,128)(2,1)S(1)} collective-permute-done((bf16[256,512]{1,0:T(8,128)(2,1)S(1)}, bf16[256,512]{1,0:T(8,128)(2,1)S(1)}, u32[]{:S(2)}, u32[]{:S(2)}) %collective-permute-start.11) | collective-permute-done | bytes 262176 | tf_op jit(solution)/shard_map/ppermute | solution.py:377
  73.1 0.0 collective-permute-done.10
  73.1 0.0 collective-permute-done.9
  73.1 1.8 %collective-permute-done.7.x_ref = bf16[2,64,1024]{2,1,0:T(8,128)(2,1)S(1)} collective-permute-done((bf16[2,64,1024]{2,1,0:T(8,128)(2,1)S(1)}, bf16[2,64,1024]{2,1,0:T(8,128)(2,1)S(1)}, u32[]{:S(2)}, u32[]{:S(2)}) %collective-permute-start.7) | collective-permute-done | bytes 262176 | tf_op jit(solution)/shard_map/ppermute | solution.py:337
  74.9 4.0 %collective-permute-done.8.y_ref = bf16[2,64,1024]{2,1,0:T(8,128)(2,1)S(1)} collective-permute-done((bf16[2,64,1024]{2,1,0:T(8,128)(2,1)S(1)}, bf16[2,64,1024]{2,1,0:T(8,128)(2,1)S(1)}, u32[]{:S(2)}, u32[]{:S(2)}) %collective-permute-start.8) | collective-permute-done | bytes 262176 | tf_op jit(solution)/shard_map/ppermute | solution.py:337
  78.9 0.1 convert_element_type.12
  78.9 0.1 convert_add_fusion
  79.0 1.0 fusion
  80.0 4.8 %all-to-all-start.1 = ((bf16[8,64,512]{2,1,0:T(8,128)(2,1)}), bf16[8,64,512]{2,1,0:T(8,128)(2,1)S(1)}, u32[]{:S(2)}, u32[]{:S(2)}) async-start(bf16[8,64,512]{2,1,0:T(8,128)(2,1)} %bitcast.8), calls=%async_computation.1 | async-start | bytes 1048576 | tf_op jit(solution)/shard_map/all_to_all | solution.py:390
  84.8 1.5 %unpack_rows.1 = f32[64,8192]{1,0:T(8,128)} custom-call(bf16[2,64,1024]{2,1,0:T(8,128)(2,1)S(1)} %get-tuple-element.29.dq_near, bf16[4,64,1024]{2,1,0:T(8,128)(2,1)S(1)} %collective-permute-done.6.got_ref, bf16[2,64,1024]{2,1,0:T(8,128)(2,1)S(1)} %collective-permute-done.7.x_ref, bf16[2,64,1024]{2,1,0:T(8,128)(2,1)S(1)} %collective-permute-done.8.y_ref), custom_call_target="tpu_custom_call" | custom-call | bytes 33554432 | tf_op jit(solution)/shard_map/unpack_rows/pallas_call | solution.py:320
  86.3 9.1 %all-to-all-done.1.kv_ref = bf16[8,64,512]{2,1,0:T(8,128)(2,1)S(1)} async-done(((bf16[8,64,512]{2,1,0:T(8,128)(2,1)}), bf16[8,64,512]{2,1,0:T(8,128)(2,1)S(1)}, u32[]{:S(2)}, u32[]{:S(2)}) %all-to-all-start.1) | async-done | bytes 524320 | tf_op jit(solution)/shard_map/all_to_all | solution.py:390
  95.4 0.9 unpack_keys.1
  (5 shorter events, 0.2 us)
Async XLA Ops:
  4.0 8.0 %copy-start.3 = (bf16[64,2048]{1,0:T(8,128)(2,1)S(1)}, bf16[64,2048]{1,0:T(8,128)(2,1)}, u32[]{:S(2)}) copy-start(bf16[64,2048]{1,0:T(8,128)(2,1)} %get-tuple-element.24) | copy-start | bytes 786436
  4.0 12.1 %copy-start.2 = (bf16[64,2048]{1,0:T(8,128)(2,1)S(1)}, bf16[64,2048]{1,0:T(8,128)(2,1)}, u32[]{:S(2)}) copy-start(bf16[64,2048]{1,0:T(8,128)(2,1)} %get-tuple-element.26) | copy-start | bytes 786436
  4.0 7.9 %collective-permute-start = (bf16[4,64,2048]{2,1,0:T(8,128)(2,1)}, bf16[4,64,2048]{2,1,0:T(8,128)(2,1)S(1)}, u32[]{:S(2)}, u32[]{:S(2)}) collective-permute-start(bf16[4,64,2048]{2,1,0:T(8,128)(2,1)} %get-tuple-element.25), channel_id=1, source_target_pairs={{0,1},{1,0},{2,3},{3,2},{4,5},{5,4},{6,7},{7,6},{8,9},{9,8},{10,11... | collective-permute-start | bytes 3145736 | tf_op jit(solution)/shard_map/ppermute | solution.py:337
  6.7 16.3 %all-to-all-start = ((bf16[8,64,512]{2,1,0:T(8,128)(2,1)}), bf16[8,64,512]{2,1,0:T(8,128)(2,1)S(1)}, u32[]{:S(2)}, u32[]{:S(2)}) async-start(bf16[8,64,512]{2,1,0:T(8,128)(2,1)} %get-tuple-element.28), calls=%async_computation | async-start | bytes 1048576 | tf_op jit(solution)/shard_map/all_to_all | solution.py:346
  11.9 35.7 %copy-start = (bf16[2,64,2048]{2,1,0:T(8,128)(2,1)S(1)}, bf16[2,64,2048]{2,1,0:T(8,128)(2,1)}, u32[]{:S(2)}) copy-start(bf16[2,64,2048]{2,1,0:T(8,128)(2,1)} %get-tuple-element.27.keep_ref) | copy-start | bytes 1572868
  11.9 35.7 %copy-start.1 = (s32[32768]{0:T(1024)S(1)}, s32[32768]{0:T(1024)}, u32[]{:S(2)}) copy-start(s32[32768]{0:T(1024)} %param.9) | copy-start | bytes 393220
  12.9 34.8 %collective-permute-start.1 = (bf16[2,64,2048]{2,1,0:T(8,128)(2,1)}, bf16[2,64,2048]{2,1,0:T(8,128)(2,1)S(1)}, u32[]{:S(2)}, u32[]{:S(2)}) collective-permute-start(bf16[2,64,2048]{2,1,0:T(8,128)(2,1)} %pad_maximum_fusion), channel_id=1, source_target_pairs={{0,128},{128,0},{1,129},{129,1},{2,130},{130,2},{3,131},{131,3},{4... | collective-permute-start | bytes 1572872 | tf_op jit(solution)/shard_map/ppermute | solution.py:337
  17.0 30.6 %collective-permute-start.2 = (bf16[2,64,2048]{2,1,0:T(8,128)(2,1)}, bf16[2,64,2048]{2,1,0:T(8,128)(2,1)S(1)}, u32[]{:S(2)}, u32[]{:S(2)}) collective-permute-start(bf16[2,64,2048]{2,1,0:T(8,128)(2,1)} %pad_maximum_fusion.1), channel_id=1, source_target_pairs={{0,64},{64,0},{1,65},{65,1},{2,66},{66,2},{3,67},{67,3},{4,68},{68... | collective-permute-start | bytes 1572872 | tf_op jit(solution)/shard_map/ppermute | solution.py:337
  23.0 3.3 %collective-permute-start.5 = (bf16[256,512]{1,0:T(8,128)(2,1)S(1)}, bf16[256,512]{1,0:T(8,128)(2,1)S(1)}, u32[]{:S(2)}, u32[]{:S(2)}) collective-permute-start(bf16[256,512]{1,0:T(8,128)(2,1)S(1)} %bitcast.17), channel_id=1, source_target_pairs={{62,446},{190,318},{63,447},{191,319},{126,510},{254,382},{127,511... | collective-permute-start | bytes 786440 | tf_op jit(solution)/shard_map/ppermute | solution.py:354
  23.7 20.4 %collective-permute-start.4 = (bf16[256,512]{1,0:T(8,128)(2,1)S(1)}, bf16[256,512]{1,0:T(8,128)(2,1)S(1)}, u32[]{:S(2)}, u32[]{:S(2)}) collective-permute-start(bf16[256,512]{1,0:T(8,128)(2,1)S(1)} %bitcast.15), channel_id=1, source_target_pairs={{62,446},{318,256},{190,318},{446,384},{63,447},{319,257},{191,319... | collective-permute-start | bytes 786440 | tf_op jit(solution)/shard_map/ppermute | solution.py:353
  25.0 22.6 %collective-permute-start.3 = (bf16[256,512]{1,0:T(8,128)(2,1)S(1)}, bf16[256,512]{1,0:T(8,128)(2,1)S(1)}, u32[]{:S(2)}, u32[]{:S(2)}) collective-permute-start(bf16[256,512]{1,0:T(8,128)(2,1)S(1)} %bitcast.16), channel_id=1, source_target_pairs={{0,2},{2,4},{4,6},{6,8},{8,10},{10,12},{12,14},{14,16},{16,18},{18... | collective-permute-start | bytes 786440 | tf_op jit(solution)/shard_map/ppermute | solution.py:352
  57.0 8.3 %collective-permute-start.6 = (bf16[4,64,1024]{2,1,0:T(8,128)(2,1)S(1)}, bf16[4,64,1024]{2,1,0:T(8,128)(2,1)S(1)}, u32[]{:S(2)}, u32[]{:S(2)}) collective-permute-start(bf16[4,64,1024]{2,1,0:T(8,128)(2,1)S(1)} %get-tuple-element.30), channel_id=1, source_target_pairs={{0,1},{1,0},{2,3},{3,2},{4,5},{5,4},{6,7},{7,6},{8,9},{9,8},{10,11... | collective-permute-start | bytes 1572872 | tf_op jit(solution)/shard_map/ppermute | solution.py:337
  59.6 13.5 %collective-permute-start.10 = (bf16[256,512]{1,0:T(8,128)(2,1)S(1)}, bf16[256,512]{1,0:T(8,128)(2,1)S(1)}, u32[]{:S(2)}, u32[]{:S(2)}) collective-permute-start(bf16[256,512]{1,0:T(8,128)(2,1)S(1)} %get-tuple-element.33), channel_id=1, source_target_pairs={{446,62},{318,190},{447,63},{319,191},{510,126},{382,254},{511,127... | collective-permute-start | bytes 786440 | tf_op jit(solution)/shard_map/ppermute | solution.py:376
  60.3 12.8 %collective-permute-start.9 = (bf16[256,512]{1,0:T(8,128)(2,1)S(1)}, bf16[256,512]{1,0:T(8,128)(2,1)S(1)}, u32[]{:S(2)}, u32[]{:S(2)}) collective-permute-start(bf16[256,512]{1,0:T(8,128)(2,1)S(1)} %get-tuple-element.33), channel_id=1, source_target_pairs={{2,0},{4,2},{6,4},{8,6},{10,8},{12,10},{14,12},{16,14},{18,16},{20... | collective-permute-start | bytes 786440 | tf_op jit(solution)/shard_map/ppermute | solution.py:375
  61.8 11.3 %collective-permute-start.11 = (bf16[256,512]{1,0:T(8,128)(2,1)S(1)}, bf16[256,512]{1,0:T(8,128)(2,1)S(1)}, u32[]{:S(2)}, u32[]{:S(2)}) collective-permute-start(bf16[256,512]{1,0:T(8,128)(2,1)S(1)} %get-tuple-element.34), channel_id=1, source_target_pairs={{446,62},{256,318},{318,190},{384,446},{447,63},{257,319},{319,191... | collective-permute-start | bytes 786440 | tf_op jit(solution)/shard_map/ppermute | solution.py:377
  65.4 9.5 %collective-permute-start.7 = (bf16[2,64,1024]{2,1,0:T(8,128)(2,1)S(1)}, bf16[2,64,1024]{2,1,0:T(8,128)(2,1)S(1)}, u32[]{:S(2)}, u32[]{:S(2)}) collective-permute-start(bf16[2,64,1024]{2,1,0:T(8,128)(2,1)S(1)} %pad_maximum_fusion.2), channel_id=1, source_target_pairs={{0,128},{128,0},{1,129},{129,1},{2,130},{130,2},{3,131},{131,3},{4... | collective-permute-start | bytes 786440 | tf_op jit(solution)/shard_map/ppermute | solution.py:337
  68.2 10.7 %collective-permute-start.8 = (bf16[2,64,1024]{2,1,0:T(8,128)(2,1)S(1)}, bf16[2,64,1024]{2,1,0:T(8,128)(2,1)S(1)}, u32[]{:S(2)}, u32[]{:S(2)}) collective-permute-start(bf16[2,64,1024]{2,1,0:T(8,128)(2,1)S(1)} %pad_maximum_fusion.3), channel_id=1, source_target_pairs={{0,64},{64,0},{1,65},{65,1},{2,66},{66,2},{3,67},{67,3},{4,68},{68... | collective-permute-start | bytes 786440 | tf_op jit(solution)/shard_map/ppermute | solution.py:337
  80.0 15.4 %all-to-all-start.1 = ((bf16[8,64,512]{2,1,0:T(8,128)(2,1)}), bf16[8,64,512]{2,1,0:T(8,128)(2,1)S(1)}, u32[]{:S(2)}, u32[]{:S(2)}) async-start(bf16[8,64,512]{2,1,0:T(8,128)(2,1)} %bitcast.8), calls=%async_computation.1 | async-start | bytes 1048576 | tf_op jit(solution)/shard_map/all_to_all | solution.py:390

commit v3 on v2

--- a/solution.py
+++ b/solution.py
@@ -75,28 +75,40 @@
     return x_head(lab, core), x_head(1 - lab, core), y_head(yh, core), y_head(1 - yh, core)
 
 
-def pack_kernel(k_ref, v_ref, q_ref, g_ref, kv_ref, keep_ref, swap_ref, x_ref, y_ref):
-    late = lax.axis_index("xh")
-    for core in (0, 1):
+def pack_kernel(
+    q_ref, g_ref, k_ref, v_ref, kv_ref, keep_ref, swap_ref, x_ref, y_ref, arrived
+):
+    late, core = lax.axis_index("xh"), lax.axis_index("core")
+    near = (keep_ref.at[0], x_ref, keep_ref.at[1], y_ref)
+    copies = []
+    for bit, outs in ((1 - core, [swap_ref.at[i] for i in range(4)]), (core, near)):
+        for out, head in zip(outs, kinds(bit)):
+            for ref, at in ((q_ref, 0), (g_ref, WIDE)):
+                copies.append(
+                    pltpu.make_async_copy(
+                        ref.at[:, span(head * WIDE, WIDE)],
+                        out.at[:, pl.ds(at, WIDE)],
+                        arrived.at[len(copies)],
+                    )
+                )
+    for copy in copies:
+        copy.start()
+    for to in (0, 1):
         for xl in (0, 1):
             for yh in (0, 1):
-                d = core * 4 + xl * 2 + yh
-                hx = x_head(jnp.where(late == 1, 1 - xl, xl), core)
-                hy = y_head(yh, core)
+                d = to * 4 + xl * 2 + yh
+                hx = x_head(jnp.where(late == 1, 1 - xl, xl), to)
+                hy = y_head(yh, to)
                 kv_ref[d, :, 0:DH] = k_ref[:, span(hx * DH, DH)]
                 kv_ref[d, :, DH : 2 * DH] = v_ref[:, span(hx * DH, DH)]
                 kv_ref[d, :, 2 * DH : 3 * DH] = k_ref[:, hy * DH : hy * DH + DH]
                 kv_ref[d, :, 3 * DH : 4 * DH] = v_ref[:, hy * DH : hy * DH + DH]
-    core = lax.axis_index("core")
-    near = (keep_ref.at[0], x_ref, keep_ref.at[1], y_ref)
-    for bit, outs in ((1 - core, [swap_ref.at[i] for i in range(4)]), (core, near)):
-        for out, head in zip(outs, kinds(bit)):
-            out[:, 0:WIDE] = q_ref[:, span(head * WIDE, WIDE)]
-            out[:, WIDE : 2 * WIDE] = g_ref[:, span(head * WIDE, WIDE)]
+    for copy in copies:
+        copy.wait()
 
 
 def attend_kernel(
-    x_ref, y_ref, keep_ref, got_ref, own_ref, prev_ref, odd_ref, even_ref, seg_ref,
+    y_ref, x_ref, keep_ref, got_ref, own_ref, even_ref, odd_ref, prev_ref, seg_ref,
     dq_near, dq_swap, dq_x, dq_y, down_ref, dnear_ref, dfar_ref,
     rows, dq, kv, kt, acc, bias, arrived,
 ):
@@ -284,7 +296,7 @@
         give(dfar_ref, FAR, 256)
 
 
-def unpack_rows_kernel(dq_near, got_ref, x_ref, y_ref, q_out):
+def unpack_rows_kernel(dq_near, got_ref, y_ref, x_ref, q_out):
     _, _, _, yh, core, lab = labels()
 
     def put(head, block):
@@ -340,8 +352,9 @@
     two = ((2, ROWS, 2 * WIDE), low)
     one = ((ROWS, 2 * WIDE), low)
     kv, keep, sent, x_rows, y_rows = call(
-        pack_kernel, "pack", (key_states, value_states, queries, out_grads),
-        [((8, ROWS, 4 * DH), low), two, four, one, one], limit=60,
+        pack_kernel, "pack", (queries, out_grads, key_states, value_states),
+        [((8, ROWS, 4 * DH), low), two, four, one, one],
+        scratch=[pltpu.SemaphoreType.DMA((16,))], limit=60, outside=2,
     )
     kv = lax.all_to_all(kv, TEAM, 0, 0, tiled=True).reshape(512, 4 * DH)
     got = swap(sent, "core")
@@ -359,7 +372,7 @@
     four = ((4, ROWS, WIDE), low)
     dq_near, sent, dq_x, dq_y, down, dnear, dfar = call(
         attend_kernel, "attend",
-        (x_rows, y_rows, keep, got, kv, kv_prev, kv_odd, kv_even, seg),
+        (y_rows, x_rows, keep, got, kv, kv_even, kv_odd, kv_prev, seg),
         [two, four, one, one, ((512, 4 * DH), wide)] + [((256, 4 * DH), low)] * 2,
         scratch=[
             pltpu.VMEM((2, 2, 2, ROWS, 2 * WIDE), low),
@@ -380,8 +393,8 @@
     dq_y = jnp.stack([dq_y, got[3]])
     dq_x = swap(dq_x, "xl")
     dq_y = swap(dq_y, "yh")
-    dq_x, dq_y, from_next, from_even, from_odd = lax.optimization_barrier(
-        (dq_x, dq_y, from_next, from_even, from_odd)
+    dq_y, dq_x, from_even, from_odd, from_next = lax.optimization_barrier(
+        (dq_y, dq_x, from_even, from_odd, from_next)
     )
     add = jnp.concatenate(
         [from_even.astype(wide), from_next.astype(wide) + from_odd.astype(wide)], axis=0
@@ -389,7 +402,7 @@
     total = (down + add).astype(low).reshape(HK, ROWS, 4 * DH)
     total = lax.all_to_all(total, TEAM, 0, 0, tiled=True)
     (query_grads,) = call(
-        unpack_rows_kernel, "unpack_rows", (dq_near, got, dq_x, dq_y),
+        unpack_rows_kernel, "unpack_rows", (dq_near, got, dq_y, dq_x),
         [((ROWS, HQ * DH), wide)], moved=32 * 2**20,
     )
     query_grads, total = lax.optimization_barrier((query_grads, total))

time: 96.8 us -> 97.1 us (level)
  waiting for transfers between devices: 39.5 us -> 37.7 us
  starting transfers between devices: 38 us -> 39.1 us
    ppermute x1, waiting for transfers between devices: 3.54 us -> 21.5 us  [on_device(): kv_prev = lax.ppermute(kv[STRETCH:], CHAIN, odd)]
    ppermute x1, waiting for transfers between devices: 17.8 us -> 0.01 us  [on_device(): kv_odd = lax.ppermute(kv[STRETCH:], CHAIN, odd_extra)]
    ppermute x6, waiting for transfers between devices: 5.78 us -> 4.5 us  [swap(): return lax.ppermute(array, axis, [(0, 1), (1, 0)])]
    ppermute x6, starting transfers between devices: 18.9 us -> 19.9 us  [swap(): return lax.ppermute(array, axis, [(0, 1), (1, 0)])]
  transfers between devices with their start and end apart: 14 -> 14, of which waited for: 7 -> 6; matrix products, arithmetic and copies ran while one was open for 2% -> 2% of each run, Pallas kernels for 2% -> 2%
where the time goes in v3:
time: 97.1 us; the launch traced here: 96.5 us
  starting transfers between devices  39.1 us (40%)
  waiting for transfers between devices  37.7 us (39%)
  Pallas kernels  15.9 us (16%)
  other arithmetic  2.83 us (3%)
    ppermute x1, waiting for transfers between devices, on_device(): kv_prev = lax.ppermute(kv[STRETCH:], CHAIN, odd)  21.5 us
    ppermute x6, starting transfers between devices, swap(): return lax.ppermute(array, axis, [(0, 1), (1, 0)])  19.9 us
    pallas_call x4, Pallas kernels, call(): pl.pallas_call(kernel, out_shape=tuple((jax.ShapeDtypeStruct(s, d) for s,...  15.9 us
    all_to_all x1, waiting for transfers between devices, on_device(): total = lax.all_to_all(total, TEAM, 0, 0, tiled=True)  9.09 us
    all_to_all x1, starting transfers between devices, on_device(): total = lax.all_to_all(total, TEAM, 0, 0, tiled=True)  5.73 us
    all_to_all x1, starting transfers between devices, on_device(): kv = lax.all_to_all(kv, TEAM, 0, 0, tiled=True).reshape(512, 4 * DH)  5.23 us
    ppermute x6, waiting for transfers between devices, swap(): return lax.ppermute(array, axis, [(0, 1), (1, 0)])  4.5 us
    ppermute x1, starting transfers between devices, on_device(): from_odd = lax.ppermute(dfar, CHAIN, back(odd_extra))  2.92 us
  transfers between devices with their start and end apart: 14, of which 6 were waited for; matrix products, arithmetic and copies ran while one was open for 2% of the time, Pallas kernels for 2%

profile of v3, /device:TPU:5, one launch (start us, length us, event | category | flops | bytes accessed | tf_op | source)
XLA Modules:
  0.0 96.5 jit_solution(13201896410093146908)
XLA Ops:
  0.6 4.2 %pack.1 = (bf16[8,64,512]{2,1,0:T(8,128)(2,1)}, bf16[2,64,2048]{2,1,0:T(8,128)(2,1)}, bf16[4,64,2048]{2,1,0:T(8,128)(2,1)}, bf16[64,2048]{1,0:T(8,128)(2,1)}, bf16[64,2048]{1,0:T(8,128)(2,1)}) custom-call(bf16[64,8192]{1,0:T(8,128)(2,1)} %q_ref.1, bf16[64,8192]{1,0:T(8,128)(2,1)} %g_ref.1, bf16[64,1024]{1,0:T(8,128)(2,1)} %k_ref.1, bf16[64,1024]{1,0:T(8,128)(2,1)} %v_ref.1), custom_call_target="tpu_custom_call" | custom-call | bytes 1024 | tf_op jit(solution)/shard_map/pack/pallas_call | solution.py:332
  4.9 0.0 copy-start.3
  4.9 0.0 copy-start.2
  4.9 2.7 %collective-permute-start = (bf16[4,64,2048]{2,1,0:T(8,128)(2,1)}, bf16[4,64,2048]{2,1,0:T(8,128)(2,1)S(1)}, u32[]{:S(2)}, u32[]{:S(2)}) collective-permute-start(bf16[4,64,2048]{2,1,0:T(8,128)(2,1)} %get-tuple-element.25), channel_id=1, source_target_pairs={{0,1},{1,0},{2,3},{3,2},{4,5},{5,4},{6,7},{7,6},{8,9},{9,8},{10,11... | collective-permute-start | bytes 3145736 | tf_op jit(solution)/shard_map/ppermute | solution.py:349
  7.6 5.2 %all-to-all-start = ((bf16[8,64,512]{2,1,0:T(8,128)(2,1)}), bf16[8,64,512]{2,1,0:T(8,128)(2,1)S(1)}, u32[]{:S(2)}, u32[]{:S(2)}) async-start(bf16[8,64,512]{2,1,0:T(8,128)(2,1)} %get-tuple-element.28), calls=%async_computation | async-start | bytes 1048576 | tf_op jit(solution)/shard_map/all_to_all | solution.py:359
  12.9 0.0 copy-start
  12.9 0.0 copy-start.1
  12.9 0.0 collective-permute-done.got_ref
  12.9 0.0 copy-done.3
  12.9 0.8 pad_maximum_fusion
  13.8 4.8 %collective-permute-start.1 = (bf16[2,64,2048]{2,1,0:T(8,128)(2,1)}, bf16[2,64,2048]{2,1,0:T(8,128)(2,1)S(1)}, u32[]{:S(2)}, u32[]{:S(2)}) collective-permute-start(bf16[2,64,2048]{2,1,0:T(8,128)(2,1)} %pad_maximum_fusion), channel_id=1, source_target_pairs={{0,64},{64,0},{1,65},{65,1},{2,66},{66,2},{3,67},{67,3},{4,68},{68... | collective-permute-start | bytes 1572872 | tf_op jit(solution)/shard_map/ppermute | solution.py:349
  18.6 0.0 copy-done.2
  18.6 0.9 pad_maximum_fusion.1
  19.4 3.1 %collective-permute-start.2 = (bf16[2,64,2048]{2,1,0:T(8,128)(2,1)}, bf16[2,64,2048]{2,1,0:T(8,128)(2,1)S(1)}, u32[]{:S(2)}, u32[]{:S(2)}) collective-permute-start(bf16[2,64,2048]{2,1,0:T(8,128)(2,1)} %pad_maximum_fusion.1), channel_id=1, source_target_pairs={{0,128},{128,0},{1,129},{129,1},{2,130},{130,2},{3,131},{131,3},{4... | collective-permute-start | bytes 1572872 | tf_op jit(solution)/shard_map/ppermute | solution.py:349
  22.5 1.0 %all-to-all-done = bf16[8,64,512]{2,1,0:T(8,128)(2,1)S(1)} async-done(((bf16[8,64,512]{2,1,0:T(8,128)(2,1)}), bf16[8,64,512]{2,1,0:T(8,128)(2,1)S(1)}, u32[]{:S(2)}, u32[]{:S(2)}) %all-to-all-start) | async-done | bytes 524320 | tf_op jit(solution)/shard_map/all_to_all | solution.py:359
  23.6 0.7 collective-permute-start.3
  24.2 1.3 %collective-permute-start.5 = (bf16[256,512]{1,0:T(8,128)(2,1)S(1)}, bf16[256,512]{1,0:T(8,128)(2,1)S(1)}, u32[]{:S(2)}, u32[]{:S(2)}) collective-permute-start(bf16[256,512]{1,0:T(8,128)(2,1)S(1)} %bitcast.15), channel_id=1, source_target_pairs={{0,2},{2,4},{4,6},{6,8},{8,10},{10,12},{12,14},{14,16},{16,18},{18... | collective-permute-start | bytes 786440 | tf_op jit(solution)/shard_map/ppermute | solution.py:365
  25.5 1.3 %collective-permute-start.4 = (bf16[256,512]{1,0:T(8,128)(2,1)S(1)}, bf16[256,512]{1,0:T(8,128)(2,1)S(1)}, u32[]{:S(2)}, u32[]{:S(2)}) collective-permute-start(bf16[256,512]{1,0:T(8,128)(2,1)S(1)} %bitcast.16), channel_id=1, source_target_pairs={{62,446},{318,256},{190,318},{446,384},{63,447},{319,257},{191,319... | collective-permute-start | bytes 786440 | tf_op jit(solution)/shard_map/ppermute | solution.py:366
  26.8 0.0 collective-permute-done.3.even_ref
  26.9 21.5 %collective-permute-done.5.prev_ref = bf16[256,512]{1,0:T(8,128)(2,1)S(1)} collective-permute-done((bf16[256,512]{1,0:T(8,128)(2,1)S(1)}, bf16[256,512]{1,0:T(8,128)(2,1)S(1)}, u32[]{:S(2)}, u32[]{:S(2)}) %collective-permute-start.5) | collective-permute-done | bytes 262176 | tf_op jit(solution)/shard_map/ppermute | solution.py:365
  48.3 0.0 collective-permute-done.4.odd_ref
  48.3 0.0 collective-permute-done.1.y_ref
  48.3 0.0 collective-permute-done.2.x_ref
  48.4 0.0 copy-done
  48.4 0.0 copy-done.1
  48.4 9.3 %attend.1 = (bf16[2,64,1024]{2,1,0:T(8,128)(2,1)S(1)}, bf16[4,64,1024]{2,1,0:T(8,128)(2,1)S(1)}, bf16[64,1024]{1,0:T(8,128)(2,1)S(1)}, bf16[64,1024]{1,0:T(8,128...) custom-call(bf16[2,64,2048]{2,1,0:T(8,128)(2,1)S(1)} %collective-permute-done.1.y_ref, ...), custom_call_target="tpu_custom_call" | custom-call | bytes 1024 | tf_op jit(solution)/shard_map/attend/pallas_call | solution.py:332
  57.7 3.2 %collective-permute-start.6 = (bf16[4,64,1024]{2,1,0:T(8,128)(2,1)S(1)}, bf16[4,64,1024]{2,1,0:T(8,128)(2,1)S(1)}, u32[]{:S(2)}, u32[]{:S(2)}) collective-permute-start(bf16[4,64,1024]{2,1,0:T(8,128)(2,1)S(1)} %get-tuple-element.30), channel_id=1, source_target_pairs={{0,1},{1,0},{2,3},{3,2},{4,5},{5,4},{6,7},{7,6},{8,9},{9,8},{10,11... | collective-permute-start | bytes 1572872 | tf_op jit(solution)/shard_map/ppermute | solution.py:349
  60.9 1.3 %collective-permute-start.11 = (bf16[256,512]{1,0:T(8,128)(2,1)S(1)}, bf16[256,512]{1,0:T(8,128)(2,1)S(1)}, u32[]{:S(2)}, u32[]{:S(2)}) collective-permute-start(bf16[256,512]{1,0:T(8,128)(2,1)S(1)} %get-tuple-element.33), channel_id=1, source_target_pairs={{2,0},{4,2},{6,4},{8,6},{10,8},{12,10},{14,12},{16,14},{18,16},{20... | collective-permute-start | bytes 786440 | tf_op jit(solution)/shard_map/ppermute | solution.py:388
  62.2 0.7 collective-permute-start.9
  62.9 2.9 %collective-permute-start.10 = (bf16[256,512]{1,0:T(8,128)(2,1)S(1)}, bf16[256,512]{1,0:T(8,128)(2,1)S(1)}, u32[]{:S(2)}, u32[]{:S(2)}) collective-permute-start(bf16[256,512]{1,0:T(8,128)(2,1)S(1)} %get-tuple-element.34), channel_id=1, source_target_pairs={{446,62},{256,318},{318,190},{384,446},{447,63},{257,319},{319,191... | collective-permute-start | bytes 786440 | tf_op jit(solution)/shard_map/ppermute | solution.py:390
  65.8 0.0 collective-permute-done.6.got_ref
  65.9 1.9 %collective-permute-start.7 = (bf16[2,64,1024]{2,1,0:T(8,128)(2,1)S(1)}, bf16[2,64,1024]{2,1,0:T(8,128)(2,1)S(1)}, u32[]{:S(2)}, u32[]{:S(2)}) collective-permute-start(bf16[2,64,1024]{2,1,0:T(8,128)(2,1)S(1)} %pad_maximum_fusion.2), channel_id=1, source_target_pairs={{0,64},{64,0},{1,65},{65,1},{2,66},{66,2},{3,67},{67,3},{4,68},{68... | collective-permute-start | bytes 786440 | tf_op jit(solution)/shard_map/ppermute | solution.py:349
  67.9 4.2 %collective-permute-start.8 = (bf16[2,64,1024]{2,1,0:T(8,128)(2,1)S(1)}, bf16[2,64,1024]{2,1,0:T(8,128)(2,1)S(1)}, u32[]{:S(2)}, u32[]{:S(2)}) collective-permute-start(bf16[2,64,1024]{2,1,0:T(8,128)(2,1)S(1)} %pad_maximum_fusion.3), channel_id=1, source_target_pairs={{0,128},{128,0},{1,129},{129,1},{2,130},{130,2},{3,131},{131,3},{4... | collective-permute-start | bytes 786440 | tf_op jit(solution)/shard_map/ppermute | solution.py:349
  72.1 1.6 %collective-permute-done.10 = bf16[256,512]{1,0:T(8,128)(2,1)S(1)} collective-permute-done((bf16[256,512]{1,0:T(8,128)(2,1)S(1)}, bf16[256,512]{1,0:T(8,128)(2,1)S(1)}, u32[]{:S(2)}, u32[]{:S(2)}) %collective-permute-start.10) | collective-permute-done | bytes 262176 | tf_op jit(solution)/shard_map/ppermute | solution.py:390
  73.7 0.0 collective-permute-done.11
  73.7 0.0 collective-permute-done.9
  73.7 3.2 %collective-permute-done.7.y_ref = bf16[2,64,1024]{2,1,0:T(8,128)(2,1)S(1)} collective-permute-done((bf16[2,64,1024]{2,1,0:T(8,128)(2,1)S(1)}, bf16[2,64,1024]{2,1,0:T(8,128)(2,1)S(1)}, u32[]{:S(2)}, u32[]{:S(2)}) %collective-permute-start.7) | collective-permute-done | bytes 262176 | tf_op jit(solution)/shard_map/ppermute | solution.py:349
  76.9 1.3 %collective-permute-done.8.x_ref = bf16[2,64,1024]{2,1,0:T(8,128)(2,1)S(1)} collective-permute-done((bf16[2,64,1024]{2,1,0:T(8,128)(2,1)S(1)}, bf16[2,64,1024]{2,1,0:T(8,128)(2,1)S(1)}, u32[]{:S(2)}, u32[]{:S(2)}) %collective-permute-start.8) | collective-permute-done | bytes 262176 | tf_op jit(solution)/shard_map/ppermute | solution.py:349
  78.2 0.1 convert_element_type.12
  78.3 0.1 convert_add_fusion
  78.4 1.0 fusion
  79.3 5.7 %all-to-all-start.1 = ((bf16[8,64,512]{2,1,0:T(8,128)(2,1)}), bf16[8,64,512]{2,1,0:T(8,128)(2,1)S(1)}, u32[]{:S(2)}, u32[]{:S(2)}) async-start(bf16[8,64,512]{2,1,0:T(8,128)(2,1)} %bitcast.8), calls=%async_computation.1 | async-start | bytes 1048576 | tf_op jit(solution)/shard_map/all_to_all | solution.py:403
  85.1 1.5 %unpack_rows.1 = f32[64,8192]{1,0:T(8,128)} custom-call(bf16[2,64,1024]{2,1,0:T(8,128)(2,1)S(1)} %get-tuple-element.29.dq_near, bf16[4,64,1024]{2,1,0:T(8,128)(2,1)S(1)} %collective-permute-done.6.got_ref, bf16[2,64,1024]{2,1,0:T(8,128)(2,1)S(1)} %collective-permute-done.7.y_ref, bf16[2,64,1024]{2,1,0:T(8,128)(2,1)S(1)} %collective-permute-done.8.x_ref), custom_call_target="tpu_custom_call" | custom-call | bytes 33554432 | tf_op jit(solution)/shard_map/unpack_rows/pallas_call | solution.py:332
  86.5 9.1 %all-to-all-done.1.kv_ref = bf16[8,64,512]{2,1,0:T(8,128)(2,1)S(1)} async-done(((bf16[8,64,512]{2,1,0:T(8,128)(2,1)}), bf16[8,64,512]{2,1,0:T(8,128)(2,1)S(1)}, u32[]{:S(2)}, u32[]{:S(2)}) %all-to-all-start.1) | async-done | bytes 524320 | tf_op jit(solution)/shard_map/all_to_all | solution.py:403
  95.6 0.9 unpack_keys.1
  (5 shorter events, 0.2 us)
Async XLA Ops:
  4.9 8.0 %copy-start.3 = (bf16[64,2048]{1,0:T(8,128)(2,1)S(1)}, bf16[64,2048]{1,0:T(8,128)(2,1)}, u32[]{:S(2)}) copy-start(bf16[64,2048]{1,0:T(8,128)(2,1)} %get-tuple-element.24) | copy-start | bytes 786436
  4.9 13.7 %copy-start.2 = (bf16[64,2048]{1,0:T(8,128)(2,1)S(1)}, bf16[64,2048]{1,0:T(8,128)(2,1)}, u32[]{:S(2)}) copy-start(bf16[64,2048]{1,0:T(8,128)(2,1)} %get-tuple-element.26) | copy-start | bytes 786436
  4.9 8.0 %collective-permute-start = (bf16[4,64,2048]{2,1,0:T(8,128)(2,1)}, bf16[4,64,2048]{2,1,0:T(8,128)(2,1)S(1)}, u32[]{:S(2)}, u32[]{:S(2)}) collective-permute-start(bf16[4,64,2048]{2,1,0:T(8,128)(2,1)} %get-tuple-element.25), channel_id=1, source_target_pairs={{0,1},{1,0},{2,3},{3,2},{4,5},{5,4},{6,7},{7,6},{8,9},{9,8},{10,11... | collective-permute-start | bytes 3145736 | tf_op jit(solution)/shard_map/ppermute | solution.py:349
  7.6 15.9 %all-to-all-start = ((bf16[8,64,512]{2,1,0:T(8,128)(2,1)}), bf16[8,64,512]{2,1,0:T(8,128)(2,1)S(1)}, u32[]{:S(2)}, u32[]{:S(2)}) async-start(bf16[8,64,512]{2,1,0:T(8,128)(2,1)} %get-tuple-element.28), calls=%async_computation | async-start | bytes 1048576 | tf_op jit(solution)/shard_map/all_to_all | solution.py:359
  12.9 35.5 %copy-start = (bf16[2,64,2048]{2,1,0:T(8,128)(2,1)S(1)}, bf16[2,64,2048]{2,1,0:T(8,128)(2,1)}, u32[]{:S(2)}) copy-start(bf16[2,64,2048]{2,1,0:T(8,128)(2,1)} %get-tuple-element.27.keep_ref) | copy-start | bytes 1572868
  12.9 35.5 %copy-start.1 = (s32[32768]{0:T(1024)S(1)}, s32[32768]{0:T(1024)}, u32[]{:S(2)}) copy-start(s32[32768]{0:T(1024)} %param.9) | copy-start | bytes 393220
  13.8 34.6 %collective-permute-start.1 = (bf16[2,64,2048]{2,1,0:T(8,128)(2,1)}, bf16[2,64,2048]{2,1,0:T(8,128)(2,1)S(1)}, u32[]{:S(2)}, u32[]{:S(2)}) collective-permute-start(bf16[2,64,2048]{2,1,0:T(8,128)(2,1)} %pad_maximum_fusion), channel_id=1, source_target_pairs={{0,64},{64,0},{1,65},{65,1},{2,66},{66,2},{3,67},{67,3},{4,68},{68... | collective-permute-start | bytes 1572872 | tf_op jit(solution)/shard_map/ppermute | solution.py:349
  19.4 28.9 %collective-permute-start.2 = (bf16[2,64,2048]{2,1,0:T(8,128)(2,1)}, bf16[2,64,2048]{2,1,0:T(8,128)(2,1)S(1)}, u32[]{:S(2)}, u32[]{:S(2)}) collective-permute-start(bf16[2,64,2048]{2,1,0:T(8,128)(2,1)} %pad_maximum_fusion.1), channel_id=1, source_target_pairs={{0,128},{128,0},{1,129},{129,1},{2,130},{130,2},{3,131},{131,3},{4... | collective-permute-start | bytes 1572872 | tf_op jit(solution)/shard_map/ppermute | solution.py:349
  23.6 3.3 %collective-permute-start.3 = (bf16[256,512]{1,0:T(8,128)(2,1)S(1)}, bf16[256,512]{1,0:T(8,128)(2,1)S(1)}, u32[]{:S(2)}, u32[]{:S(2)}) collective-permute-start(bf16[256,512]{1,0:T(8,128)(2,1)S(1)} %bitcast.17), channel_id=1, source_target_pairs={{62,446},{190,318},{63,447},{191,319},{126,510},{254,382},{127,511... | collective-permute-start | bytes 786440 | tf_op jit(solution)/shard_map/ppermute | solution.py:367
  24.2 24.1 %collective-permute-start.5 = (bf16[256,512]{1,0:T(8,128)(2,1)S(1)}, bf16[256,512]{1,0:T(8,128)(2,1)S(1)}, u32[]{:S(2)}, u32[]{:S(2)}) collective-permute-start(bf16[256,512]{1,0:T(8,128)(2,1)S(1)} %bitcast.15), channel_id=1, source_target_pairs={{0,2},{2,4},{4,6},{6,8},{8,10},{10,12},{12,14},{14,16},{16,18},{18... | collective-permute-start | bytes 786440 | tf_op jit(solution)/shard_map/ppermute | solution.py:365
  25.5 22.8 %collective-permute-start.4 = (bf16[256,512]{1,0:T(8,128)(2,1)S(1)}, bf16[256,512]{1,0:T(8,128)(2,1)S(1)}, u32[]{:S(2)}, u32[]{:S(2)}) collective-permute-start(bf16[256,512]{1,0:T(8,128)(2,1)S(1)} %bitcast.16), channel_id=1, source_target_pairs={{62,446},{318,256},{190,318},{446,384},{63,447},{319,257},{191,319... | collective-permute-start | bytes 786440 | tf_op jit(solution)/shard_map/ppermute | solution.py:366
  57.7 8.2 %collective-permute-start.6 = (bf16[4,64,1024]{2,1,0:T(8,128)(2,1)S(1)}, bf16[4,64,1024]{2,1,0:T(8,128)(2,1)S(1)}, u32[]{:S(2)}, u32[]{:S(2)}) collective-permute-start(bf16[4,64,1024]{2,1,0:T(8,128)(2,1)S(1)} %get-tuple-element.30), channel_id=1, source_target_pairs={{0,1},{1,0},{2,3},{3,2},{4,5},{5,4},{6,7},{7,6},{8,9},{9,8},{10,11... | collective-permute-start | bytes 1572872 | tf_op jit(solution)/shard_map/ppermute | solution.py:349
  60.9 12.8 %collective-permute-start.11 = (bf16[256,512]{1,0:T(8,128)(2,1)S(1)}, bf16[256,512]{1,0:T(8,128)(2,1)S(1)}, u32[]{:S(2)}, u32[]{:S(2)}) collective-permute-start(bf16[256,512]{1,0:T(8,128)(2,1)S(1)} %get-tuple-element.33), channel_id=1, source_target_pairs={{2,0},{4,2},{6,4},{8,6},{10,8},{12,10},{14,12},{16,14},{18,16},{20... | collective-permute-start | bytes 786440 | tf_op jit(solution)/shard_map/ppermute | solution.py:388
  62.2 11.5 %collective-permute-start.9 = (bf16[256,512]{1,0:T(8,128)(2,1)S(1)}, bf16[256,512]{1,0:T(8,128)(2,1)S(1)}, u32[]{:S(2)}, u32[]{:S(2)}) collective-permute-start(bf16[256,512]{1,0:T(8,128)(2,1)S(1)} %get-tuple-element.33), channel_id=1, source_target_pairs={{446,62},{318,190},{447,63},{319,191},{510,126},{382,254},{511,127... | collective-permute-start | bytes 786440 | tf_op jit(solution)/shard_map/ppermute | solution.py:389
  62.9 10.8 %collective-permute-start.10 = (bf16[256,512]{1,0:T(8,128)(2,1)S(1)}, bf16[256,512]{1,0:T(8,128)(2,1)S(1)}, u32[]{:S(2)}, u32[]{:S(2)}) collective-permute-start(bf16[256,512]{1,0:T(8,128)(2,1)S(1)} %get-tuple-element.34), channel_id=1, source_target_pairs={{446,62},{256,318},{318,190},{384,446},{447,63},{257,319},{319,191... | collective-permute-start | bytes 786440 | tf_op jit(solution)/shard_map/ppermute | solution.py:390
  65.9 11.0 %collective-permute-start.7 = (bf16[2,64,1024]{2,1,0:T(8,128)(2,1)S(1)}, bf16[2,64,1024]{2,1,0:T(8,128)(2,1)S(1)}, u32[]{:S(2)}, u32[]{:S(2)}) collective-permute-start(bf16[2,64,1024]{2,1,0:T(8,128)(2,1)S(1)} %pad_maximum_fusion.2), channel_id=1, source_target_pairs={{0,64},{64,0},{1,65},{65,1},{2,66},{66,2},{3,67},{67,3},{4,68},{68... | collective-permute-start | bytes 786440 | tf_op jit(solution)/shard_map/ppermute | solution.py:349
  67.9 10.4 %collective-permute-start.8 = (bf16[2,64,1024]{2,1,0:T(8,128)(2,1)S(1)}, bf16[2,64,1024]{2,1,0:T(8,128)(2,1)S(1)}, u32[]{:S(2)}, u32[]{:S(2)}) collective-permute-start(bf16[2,64,1024]{2,1,0:T(8,128)(2,1)S(1)} %pad_maximum_fusion.3), channel_id=1, source_target_pairs={{0,128},{128,0},{1,129},{129,1},{2,130},{130,2},{3,131},{131,3},{4... | collective-permute-start | bytes 786440 | tf_op jit(solution)/shard_map/ppermute | solution.py:349
  79.3 16.3 %all-to-all-start.1 = ((bf16[8,64,512]{2,1,0:T(8,128)(2,1)}), bf16[8,64,512]{2,1,0:T(8,128)(2,1)S(1)}, u32[]{:S(2)}, u32[]{:S(2)}) async-start(bf16[8,64,512]{2,1,0:T(8,128)(2,1)} %bitcast.8), calls=%async_computation.1 | async-start | bytes 1048576 | tf_op jit(solution)/shard_map/all_to_all | solution.py:403

commit v4 on v2

--- a/solution.py
+++ b/solution.py
@@ -96,7 +96,7 @@
 
 
 def attend_kernel(
-    x_ref, y_ref, keep_ref, got_ref, own_ref, prev_ref, odd_ref, even_ref, seg_ref,
+    y_ref, x_ref, keep_ref, got_ref, own_ref, even_ref, odd_ref, prev_ref, seg_ref,
     dq_near, dq_swap, dq_x, dq_y, down_ref, dnear_ref, dfar_ref,
     rows, dq, kv, kt, acc, bias, arrived,
 ):
@@ -284,7 +284,7 @@
         give(dfar_ref, FAR, 256)
 
 
-def unpack_rows_kernel(dq_near, got_ref, x_ref, y_ref, q_out):
+def unpack_rows_kernel(dq_near, got_ref, y_ref, x_ref, q_out):
     _, _, _, yh, core, lab = labels()
 
     def put(head, block):
@@ -359,7 +359,7 @@
     four = ((4, ROWS, WIDE), low)
     dq_near, sent, dq_x, dq_y, down, dnear, dfar = call(
         attend_kernel, "attend",
-        (x_rows, y_rows, keep, got, kv, kv_prev, kv_odd, kv_even, seg),
+        (y_rows, x_rows, keep, got, kv, kv_even, kv_odd, kv_prev, seg),
         [two, four, one, one, ((512, 4 * DH), wide)] + [((256, 4 * DH), low)] * 2,
         scratch=[
             pltpu.VMEM((2, 2, 2, ROWS, 2 * WIDE), low),
@@ -380,8 +380,8 @@
     dq_y = jnp.stack([dq_y, got[3]])
     dq_x = swap(dq_x, "xl")
     dq_y = swap(dq_y, "yh")
-    dq_x, dq_y, from_next, from_even, from_odd = lax.optimization_barrier(
-        (dq_x, dq_y, from_next, from_even, from_odd)
+    dq_y, dq_x, from_even, from_odd, from_next = lax.optimization_barrier(
+        (dq_y, dq_x, from_even, from_odd, from_next)
     )
     add = jnp.concatenate(
         [from_even.astype(wide), from_next.astype(wide) + from_odd.astype(wide)], axis=0
@@ -389,7 +389,7 @@
     total = (down + add).astype(low).reshape(HK, ROWS, 4 * DH)
     total = lax.all_to_all(total, TEAM, 0, 0, tiled=True)
     (query_grads,) = call(
-        unpack_rows_kernel, "unpack_rows", (dq_near, got, dq_x, dq_y),
+        unpack_rows_kernel, "unpack_rows", (dq_near, got, dq_y, dq_x),
         [((ROWS, HQ * DH), wide)], moved=32 * 2**20,
     )
     query_grads, total = lax.optimization_barrier((query_grads, total))

time: 96.8 us -> 96.2 us (level)
  waiting for transfers between devices: 39.5 us -> 37.7 us
  starting transfers between devices: 38 us -> 39 us
    ppermute x1, waiting for transfers between devices: 3.54 us -> 21.5 us  [on_device(): kv_prev = lax.ppermute(kv[STRETCH:], CHAIN, odd)]
    ppermute x1, waiting for transfers between devices: 17.8 us -> 0.01 us  [on_device(): kv_odd = lax.ppermute(kv[STRETCH:], CHAIN, odd_extra)]
    ppermute x6, waiting for transfers between devices: 5.78 us -> 4.5 us  [swap(): return lax.ppermute(array, axis, [(0, 1), (1, 0)])]
  transfers between devices with their start and end apart: 14 -> 14, of which waited for: 7 -> 6; matrix products, arithmetic and copies ran while one was open for 2% -> 2% of each run, Pallas kernels for 2% -> 2%
where the time goes in v4:
time: 96.2 us; the launch traced here: 95.6 us
  starting transfers between devices  39 us (41%)
  waiting for transfers between devices  37.7 us (39%)
  Pallas kernels  15 us (16%)
  other arithmetic  2.83 us (3%)
    ppermute x1, waiting for transfers between devices, on_device(): kv_prev = lax.ppermute(kv[STRETCH:], CHAIN, odd)  21.5 us
    ppermute x6, starting transfers between devices, swap(): return lax.ppermute(array, axis, [(0, 1), (1, 0)])  19.9 us
    pallas_call x4, Pallas kernels, call(): pl.pallas_call(kernel, out_shape=tuple((jax.ShapeDtypeStruct(s, d) for s,...  15 us
    all_to_all x1, waiting for transfers between devices, on_device(): total = lax.all_to_all(total, TEAM, 0, 0, tiled=True)  9.09 us
    all_to_all x1, starting transfers between devices, on_device(): total = lax.all_to_all(total, TEAM, 0, 0, tiled=True)  5.74 us
    all_to_all x1, starting transfers between devices, on_device(): kv = lax.all_to_all(kv, TEAM, 0, 0, tiled=True).reshape(512, 4 * DH)  5.23 us
    ppermute x6, waiting for transfers between devices, swap(): return lax.ppermute(array, axis, [(0, 1), (1, 0)])  4.5 us
    ppermute x1, starting transfers between devices, on_device(): from_odd = lax.ppermute(dfar, CHAIN, back(odd_extra))  2.92 us
  transfers between devices with their start and end apart: 14, of which 6 were waited for; matrix products, arithmetic and copies ran while one was open for 2% of the time, Pallas kernels for 2%

profile of v4, /device:TPU:5, one launch (start us, length us, event | category | flops | bytes accessed | tf_op | source)
XLA Modules:
  0.0 95.6 jit_solution(4693074857474735830)
XLA Ops:
  0.6 3.4 %pack.1 = (bf16[8,64,512]{2,1,0:T(8,128)(2,1)}, bf16[2,64,2048]{2,1,0:T(8,128)(2,1)}, bf16[4,64,2048]{2,1,0:T(8,128)(2,1)}, bf16[64,2048]{1,0:T(8,128)(2,1)}, bf16[64,2048]{1,0:T(8,128)(2,1)}) custom-call(bf16[64,1024]{1,0:T(8,128)(2,1)} %k_ref.1, bf16[64,1024]{1,0:T(8,128)(2,1)} %v_ref.1, bf16[64,8192]{1,0:T(8,128)(2,1)} %q_ref.1, bf16[64,8192]{1,0:T(8,128)(2,1)} %g_ref.1), custom_call_target="tpu_custom_call" | custom-call | bytes 1024 | tf_op jit(solution)/shard_map/pack/pallas_call | solution.py:320
  4.0 0.0 copy-start.3
  4.0 0.0 copy-start.2
  4.0 2.7 %collective-permute-start = (bf16[4,64,2048]{2,1,0:T(8,128)(2,1)}, bf16[4,64,2048]{2,1,0:T(8,128)(2,1)S(1)}, u32[]{:S(2)}, u32[]{:S(2)}) collective-permute-start(bf16[4,64,2048]{2,1,0:T(8,128)(2,1)} %get-tuple-element.25), channel_id=1, source_target_pairs={{0,1},{1,0},{2,3},{3,2},{4,5},{5,4},{6,7},{7,6},{8,9},{9,8},{10,11... | collective-permute-start | bytes 3145736 | tf_op jit(solution)/shard_map/ppermute | solution.py:337
  6.7 5.2 %all-to-all-start = ((bf16[8,64,512]{2,1,0:T(8,128)(2,1)}), bf16[8,64,512]{2,1,0:T(8,128)(2,1)S(1)}, u32[]{:S(2)}, u32[]{:S(2)}) async-start(bf16[8,64,512]{2,1,0:T(8,128)(2,1)} %get-tuple-element.28), calls=%async_computation | async-start | bytes 1048576 | tf_op jit(solution)/shard_map/all_to_all | solution.py:346
  11.9 0.0 copy-start
  11.9 0.0 copy-start.1
  12.0 0.0 collective-permute-done.got_ref
  12.0 0.0 copy-done.3
  12.0 0.8 pad_maximum_fusion
  12.9 4.8 %collective-permute-start.1 = (bf16[2,64,2048]{2,1,0:T(8,128)(2,1)}, bf16[2,64,2048]{2,1,0:T(8,128)(2,1)S(1)}, u32[]{:S(2)}, u32[]{:S(2)}) collective-permute-start(bf16[2,64,2048]{2,1,0:T(8,128)(2,1)} %pad_maximum_fusion), channel_id=1, source_target_pairs={{0,64},{64,0},{1,65},{65,1},{2,66},{66,2},{3,67},{67,3},{4,68},{68... | collective-permute-start | bytes 1572872 | tf_op jit(solution)/shard_map/ppermute | solution.py:337
  17.6 0.0 copy-done.2
  17.7 0.9 pad_maximum_fusion.1
  18.5 3.1 %collective-permute-start.2 = (bf16[2,64,2048]{2,1,0:T(8,128)(2,1)}, bf16[2,64,2048]{2,1,0:T(8,128)(2,1)S(1)}, u32[]{:S(2)}, u32[]{:S(2)}) collective-permute-start(bf16[2,64,2048]{2,1,0:T(8,128)(2,1)} %pad_maximum_fusion.1), channel_id=1, source_target_pairs={{0,128},{128,0},{1,129},{129,1},{2,130},{130,2},{3,131},{131,3},{4... | collective-permute-start | bytes 1572872 | tf_op jit(solution)/shard_map/ppermute | solution.py:337
  21.6 1.0 %all-to-all-done = bf16[8,64,512]{2,1,0:T(8,128)(2,1)S(1)} async-done(((bf16[8,64,512]{2,1,0:T(8,128)(2,1)}), bf16[8,64,512]{2,1,0:T(8,128)(2,1)S(1)}, u32[]{:S(2)}, u32[]{:S(2)}) %all-to-all-start) | async-done | bytes 524320 | tf_op jit(solution)/shard_map/all_to_all | solution.py:346
  22.7 0.7 collective-permute-start.3
  23.3 1.3 %collective-permute-start.5 = (bf16[256,512]{1,0:T(8,128)(2,1)S(1)}, bf16[256,512]{1,0:T(8,128)(2,1)S(1)}, u32[]{:S(2)}, u32[]{:S(2)}) collective-permute-start(bf16[256,512]{1,0:T(8,128)(2,1)S(1)} %bitcast.15), channel_id=1, source_target_pairs={{0,2},{2,4},{4,6},{6,8},{8,10},{10,12},{12,14},{14,16},{16,18},{18... | collective-permute-start | bytes 786440 | tf_op jit(solution)/shard_map/ppermute | solution.py:352
  24.6 1.3 %collective-permute-start.4 = (bf16[256,512]{1,0:T(8,128)(2,1)S(1)}, bf16[256,512]{1,0:T(8,128)(2,1)S(1)}, u32[]{:S(2)}, u32[]{:S(2)}) collective-permute-start(bf16[256,512]{1,0:T(8,128)(2,1)S(1)} %bitcast.16), channel_id=1, source_target_pairs={{62,446},{318,256},{190,318},{446,384},{63,447},{319,257},{191,319... | collective-permute-start | bytes 786440 | tf_op jit(solution)/shard_map/ppermute | solution.py:353
  25.9 0.0 collective-permute-done.3.even_ref
  26.0 21.5 %collective-permute-done.5.prev_ref = bf16[256,512]{1,0:T(8,128)(2,1)S(1)} collective-permute-done((bf16[256,512]{1,0:T(8,128)(2,1)S(1)}, bf16[256,512]{1,0:T(8,128)(2,1)S(1)}, u32[]{:S(2)}, u32[]{:S(2)}) %collective-permute-start.5) | collective-permute-done | bytes 262176 | tf_op jit(solution)/shard_map/ppermute | solution.py:352
  47.4 0.0 collective-permute-done.4.odd_ref
  47.4 0.0 collective-permute-done.1.y_ref
  47.4 0.0 collective-permute-done.2.x_ref
  47.4 0.0 copy-done
  47.5 0.0 copy-done.1
  47.5 9.3 %attend.1 = (bf16[2,64,1024]{2,1,0:T(8,128)(2,1)S(1)}, bf16[4,64,1024]{2,1,0:T(8,128)(2,1)S(1)}, bf16[64,1024]{1,0:T(8,128)(2,1)S(1)}, bf16[64,1024]{1,0:T(8,128...) custom-call(bf16[2,64,2048]{2,1,0:T(8,128)(2,1)S(1)} %collective-permute-done.1.y_ref, ...), custom_call_target="tpu_custom_call" | custom-call | bytes 1024 | tf_op jit(solution)/shard_map/attend/pallas_call | solution.py:320
  56.8 3.2 %collective-permute-start.6 = (bf16[4,64,1024]{2,1,0:T(8,128)(2,1)S(1)}, bf16[4,64,1024]{2,1,0:T(8,128)(2,1)S(1)}, u32[]{:S(2)}, u32[]{:S(2)}) collective-permute-start(bf16[4,64,1024]{2,1,0:T(8,128)(2,1)S(1)} %get-tuple-element.30), channel_id=1, source_target_pairs={{0,1},{1,0},{2,3},{3,2},{4,5},{5,4},{6,7},{7,6},{8,9},{9,8},{10,11... | collective-permute-start | bytes 1572872 | tf_op jit(solution)/shard_map/ppermute | solution.py:337
  60.0 1.3 %collective-permute-start.11 = (bf16[256,512]{1,0:T(8,128)(2,1)S(1)}, bf16[256,512]{1,0:T(8,128)(2,1)S(1)}, u32[]{:S(2)}, u32[]{:S(2)}) collective-permute-start(bf16[256,512]{1,0:T(8,128)(2,1)S(1)} %get-tuple-element.33), channel_id=1, source_target_pairs={{2,0},{4,2},{6,4},{8,6},{10,8},{12,10},{14,12},{16,14},{18,16},{20... | collective-permute-start | bytes 786440 | tf_op jit(solution)/shard_map/ppermute | solution.py:375
  61.3 0.7 collective-permute-start.9
  62.0 2.9 %collective-permute-start.10 = (bf16[256,512]{1,0:T(8,128)(2,1)S(1)}, bf16[256,512]{1,0:T(8,128)(2,1)S(1)}, u32[]{:S(2)}, u32[]{:S(2)}) collective-permute-start(bf16[256,512]{1,0:T(8,128)(2,1)S(1)} %get-tuple-element.34), channel_id=1, source_target_pairs={{446,62},{256,318},{318,190},{384,446},{447,63},{257,319},{319,191... | collective-permute-start | bytes 786440 | tf_op jit(solution)/shard_map/ppermute | solution.py:377
  64.9 0.0 collective-permute-done.6.got_ref
  65.0 1.9 %collective-permute-start.7 = (bf16[2,64,1024]{2,1,0:T(8,128)(2,1)S(1)}, bf16[2,64,1024]{2,1,0:T(8,128)(2,1)S(1)}, u32[]{:S(2)}, u32[]{:S(2)}) collective-permute-start(bf16[2,64,1024]{2,1,0:T(8,128)(2,1)S(1)} %pad_maximum_fusion.2), channel_id=1, source_target_pairs={{0,64},{64,0},{1,65},{65,1},{2,66},{66,2},{3,67},{67,3},{4,68},{68... | collective-permute-start | bytes 786440 | tf_op jit(solution)/shard_map/ppermute | solution.py:337
  67.0 4.2 %collective-permute-start.8 = (bf16[2,64,1024]{2,1,0:T(8,128)(2,1)S(1)}, bf16[2,64,1024]{2,1,0:T(8,128)(2,1)S(1)}, u32[]{:S(2)}, u32[]{:S(2)}) collective-permute-start(bf16[2,64,1024]{2,1,0:T(8,128)(2,1)S(1)} %pad_maximum_fusion.3), channel_id=1, source_target_pairs={{0,128},{128,0},{1,129},{129,1},{2,130},{130,2},{3,131},{131,3},{4... | collective-permute-start | bytes 786440 | tf_op jit(solution)/shard_map/ppermute | solution.py:337
  71.2 1.6 %collective-permute-done.10 = bf16[256,512]{1,0:T(8,128)(2,1)S(1)} collective-permute-done((bf16[256,512]{1,0:T(8,128)(2,1)S(1)}, bf16[256,512]{1,0:T(8,128)(2,1)S(1)}, u32[]{:S(2)}, u32[]{:S(2)}) %collective-permute-start.10) | collective-permute-done | bytes 262176 | tf_op jit(solution)/shard_map/ppermute | solution.py:377
  72.8 0.0 collective-permute-done.11
  72.8 0.0 collective-permute-done.9
  72.8 3.2 %collective-permute-done.7.y_ref = bf16[2,64,1024]{2,1,0:T(8,128)(2,1)S(1)} collective-permute-done((bf16[2,64,1024]{2,1,0:T(8,128)(2,1)S(1)}, bf16[2,64,1024]{2,1,0:T(8,128)(2,1)S(1)}, u32[]{:S(2)}, u32[]{:S(2)}) %collective-permute-start.7) | collective-permute-done | bytes 262176 | tf_op jit(solution)/shard_map/ppermute | solution.py:337
  76.0 1.3 %collective-permute-done.8.x_ref = bf16[2,64,1024]{2,1,0:T(8,128)(2,1)S(1)} collective-permute-done((bf16[2,64,1024]{2,1,0:T(8,128)(2,1)S(1)}, bf16[2,64,1024]{2,1,0:T(8,128)(2,1)S(1)}, u32[]{:S(2)}, u32[]{:S(2)}) %collective-permute-start.8) | collective-permute-done | bytes 262176 | tf_op jit(solution)/shard_map/ppermute | solution.py:337
  77.3 0.1 convert_element_type.12
  77.4 0.1 convert_add_fusion
  77.5 1.0 %fusion = bf16[512,512]{1,0:T(8,128)(2,1)} fusion(f32[512,512]{1,0:T(8,128)S(1)} %get-tuple-element.37, f32[256,512]{1,0:T(8,128)S(1)} %convert_add_fusion, f32[256,512]{1,0:T(8,128)S(1)} %convert_element_type.12), kind=kLoop, calls=%fused_computation.1 | loop fusion | flops 786432 | bytes 2621440 | tf_op jit(solution)/shard_map/convert_element_type | solution.py:389
  78.4 5.7 %all-to-all-start.1 = ((bf16[8,64,512]{2,1,0:T(8,128)(2,1)}), bf16[8,64,512]{2,1,0:T(8,128)(2,1)S(1)}, u32[]{:S(2)}, u32[]{:S(2)}) async-start(bf16[8,64,512]{2,1,0:T(8,128)(2,1)} %bitcast.8), calls=%async_computation.1 | async-start | bytes 1048576 | tf_op jit(solution)/shard_map/all_to_all | solution.py:390
  84.2 1.5 %unpack_rows.1 = f32[64,8192]{1,0:T(8,128)} custom-call(bf16[2,64,1024]{2,1,0:T(8,128)(2,1)S(1)} %get-tuple-element.29.dq_near, bf16[4,64,1024]{2,1,0:T(8,128)(2,1)S(1)} %collective-permute-done.6.got_ref, bf16[2,64,1024]{2,1,0:T(8,128)(2,1)S(1)} %collective-permute-done.7.y_ref, bf16[2,64,1024]{2,1,0:T(8,128)(2,1)S(1)} %collective-permute-done.8.x_ref), custom_call_target="tpu_custom_call" | custom-call | bytes 33554432 | tf_op jit(solution)/shard_map/unpack_rows/pallas_call | solution.py:320
  85.6 9.1 %all-to-all-done.1.kv_ref = bf16[8,64,512]{2,1,0:T(8,128)(2,1)S(1)} async-done(((bf16[8,64,512]{2,1,0:T(8,128)(2,1)}), bf16[8,64,512]{2,1,0:T(8,128)(2,1)S(1)}, u32[]{:S(2)}, u32[]{:S(2)}) %all-to-all-start.1) | async-done | bytes 524320 | tf_op jit(solution)/shard_map/all_to_all | solution.py:390
  94.7 0.9 unpack_keys.1
  (5 shorter events, 0.2 us)
Async XLA Ops:
  4.0 8.0 %copy-start.3 = (bf16[64,2048]{1,0:T(8,128)(2,1)S(1)}, bf16[64,2048]{1,0:T(8,128)(2,1)}, u32[]{:S(2)}) copy-start(bf16[64,2048]{1,0:T(8,128)(2,1)} %get-tuple-element.24) | copy-start | bytes 786436
  4.0 13.6 %copy-start.2 = (bf16[64,2048]{1,0:T(8,128)(2,1)S(1)}, bf16[64,2048]{1,0:T(8,128)(2,1)}, u32[]{:S(2)}) copy-start(bf16[64,2048]{1,0:T(8,128)(2,1)} %get-tuple-element.26) | copy-start | bytes 786436
  4.0 7.9 %collective-permute-start = (bf16[4,64,2048]{2,1,0:T(8,128)(2,1)}, bf16[4,64,2048]{2,1,0:T(8,128)(2,1)S(1)}, u32[]{:S(2)}, u32[]{:S(2)}) collective-permute-start(bf16[4,64,2048]{2,1,0:T(8,128)(2,1)} %get-tuple-element.25), channel_id=1, source_target_pairs={{0,1},{1,0},{2,3},{3,2},{4,5},{5,4},{6,7},{7,6},{8,9},{9,8},{10,11... | collective-permute-start | bytes 3145736 | tf_op jit(solution)/shard_map/ppermute | solution.py:337
  6.7 15.9 %all-to-all-start = ((bf16[8,64,512]{2,1,0:T(8,128)(2,1)}), bf16[8,64,512]{2,1,0:T(8,128)(2,1)S(1)}, u32[]{:S(2)}, u32[]{:S(2)}) async-start(bf16[8,64,512]{2,1,0:T(8,128)(2,1)} %get-tuple-element.28), calls=%async_computation | async-start | bytes 1048576 | tf_op jit(solution)/shard_map/all_to_all | solution.py:346
  11.9 35.5 %copy-start = (bf16[2,64,2048]{2,1,0:T(8,128)(2,1)S(1)}, bf16[2,64,2048]{2,1,0:T(8,128)(2,1)}, u32[]{:S(2)}) copy-start(bf16[2,64,2048]{2,1,0:T(8,128)(2,1)} %get-tuple-element.27.keep_ref) | copy-start | bytes 1572868
  11.9 35.5 %copy-start.1 = (s32[32768]{0:T(1024)S(1)}, s32[32768]{0:T(1024)}, u32[]{:S(2)}) copy-start(s32[32768]{0:T(1024)} %param.9) | copy-start | bytes 393220
  12.9 34.6 %collective-permute-start.1 = (bf16[2,64,2048]{2,1,0:T(8,128)(2,1)}, bf16[2,64,2048]{2,1,0:T(8,128)(2,1)S(1)}, u32[]{:S(2)}, u32[]{:S(2)}) collective-permute-start(bf16[2,64,2048]{2,1,0:T(8,128)(2,1)} %pad_maximum_fusion), channel_id=1, source_target_pairs={{0,64},{64,0},{1,65},{65,1},{2,66},{66,2},{3,67},{67,3},{4,68},{68... | collective-permute-start | bytes 1572872 | tf_op jit(solution)/shard_map/ppermute | solution.py:337
  18.5 28.9 %collective-permute-start.2 = (bf16[2,64,2048]{2,1,0:T(8,128)(2,1)}, bf16[2,64,2048]{2,1,0:T(8,128)(2,1)S(1)}, u32[]{:S(2)}, u32[]{:S(2)}) collective-permute-start(bf16[2,64,2048]{2,1,0:T(8,128)(2,1)} %pad_maximum_fusion.1), channel_id=1, source_target_pairs={{0,128},{128,0},{1,129},{129,1},{2,130},{130,2},{3,131},{131,3},{4... | collective-permute-start | bytes 1572872 | tf_op jit(solution)/shard_map/ppermute | solution.py:337
  22.7 3.3 %collective-permute-start.3 = (bf16[256,512]{1,0:T(8,128)(2,1)S(1)}, bf16[256,512]{1,0:T(8,128)(2,1)S(1)}, u32[]{:S(2)}, u32[]{:S(2)}) collective-permute-start(bf16[256,512]{1,0:T(8,128)(2,1)S(1)} %bitcast.17), channel_id=1, source_target_pairs={{62,446},{190,318},{63,447},{191,319},{126,510},{254,382},{127,511... | collective-permute-start | bytes 786440 | tf_op jit(solution)/shard_map/ppermute | solution.py:354
  23.3 24.1 %collective-permute-start.5 = (bf16[256,512]{1,0:T(8,128)(2,1)S(1)}, bf16[256,512]{1,0:T(8,128)(2,1)S(1)}, u32[]{:S(2)}, u32[]{:S(2)}) collective-permute-start(bf16[256,512]{1,0:T(8,128)(2,1)S(1)} %bitcast.15), channel_id=1, source_target_pairs={{0,2},{2,4},{4,6},{6,8},{8,10},{10,12},{12,14},{14,16},{16,18},{18... | collective-permute-start | bytes 786440 | tf_op jit(solution)/shard_map/ppermute | solution.py:352
  24.6 22.8 %collective-permute-start.4 = (bf16[256,512]{1,0:T(8,128)(2,1)S(1)}, bf16[256,512]{1,0:T(8,128)(2,1)S(1)}, u32[]{:S(2)}, u32[]{:S(2)}) collective-permute-start(bf16[256,512]{1,0:T(8,128)(2,1)S(1)} %bitcast.16), channel_id=1, source_target_pairs={{62,446},{318,256},{190,318},{446,384},{63,447},{319,257},{191,319... | collective-permute-start | bytes 786440 | tf_op jit(solution)/shard_map/ppermute | solution.py:353
  56.8 8.1 %collective-permute-start.6 = (bf16[4,64,1024]{2,1,0:T(8,128)(2,1)S(1)}, bf16[4,64,1024]{2,1,0:T(8,128)(2,1)S(1)}, u32[]{:S(2)}, u32[]{:S(2)}) collective-permute-start(bf16[4,64,1024]{2,1,0:T(8,128)(2,1)S(1)} %get-tuple-element.30), channel_id=1, source_target_pairs={{0,1},{1,0},{2,3},{3,2},{4,5},{5,4},{6,7},{7,6},{8,9},{9,8},{10,11... | collective-permute-start | bytes 1572872 | tf_op jit(solution)/shard_map/ppermute | solution.py:337
  60.0 12.8 %collective-permute-start.11 = (bf16[256,512]{1,0:T(8,128)(2,1)S(1)}, bf16[256,512]{1,0:T(8,128)(2,1)S(1)}, u32[]{:S(2)}, u32[]{:S(2)}) collective-permute-start(bf16[256,512]{1,0:T(8,128)(2,1)S(1)} %get-tuple-element.33), channel_id=1, source_target_pairs={{2,0},{4,2},{6,4},{8,6},{10,8},{12,10},{14,12},{16,14},{18,16},{20... | collective-permute-start | bytes 786440 | tf_op jit(solution)/shard_map/ppermute | solution.py:375
  61.3 11.5 %collective-permute-start.9 = (bf16[256,512]{1,0:T(8,128)(2,1)S(1)}, bf16[256,512]{1,0:T(8,128)(2,1)S(1)}, u32[]{:S(2)}, u32[]{:S(2)}) collective-permute-start(bf16[256,512]{1,0:T(8,128)(2,1)S(1)} %get-tuple-element.33), channel_id=1, source_target_pairs={{446,62},{318,190},{447,63},{319,191},{510,126},{382,254},{511,127... | collective-permute-start | bytes 786440 | tf_op jit(solution)/shard_map/ppermute | solution.py:376
  62.0 10.8 %collective-permute-start.10 = (bf16[256,512]{1,0:T(8,128)(2,1)S(1)}, bf16[256,512]{1,0:T(8,128)(2,1)S(1)}, u32[]{:S(2)}, u32[]{:S(2)}) collective-permute-start(bf16[256,512]{1,0:T(8,128)(2,1)S(1)} %get-tuple-element.34), channel_id=1, source_target_pairs={{446,62},{256,318},{318,190},{384,446},{447,63},{257,319},{319,191... | collective-permute-start | bytes 786440 | tf_op jit(solution)/shard_map/ppermute | solution.py:377
  65.0 11.0 %collective-permute-start.7 = (bf16[2,64,1024]{2,1,0:T(8,128)(2,1)S(1)}, bf16[2,64,1024]{2,1,0:T(8,128)(2,1)S(1)}, u32[]{:S(2)}, u32[]{:S(2)}) collective-permute-start(bf16[2,64,1024]{2,1,0:T(8,128)(2,1)S(1)} %pad_maximum_fusion.2), channel_id=1, source_target_pairs={{0,64},{64,0},{1,65},{65,1},{2,66},{66,2},{3,67},{67,3},{4,68},{68... | collective-permute-start | bytes 786440 | tf_op jit(solution)/shard_map/ppermute | solution.py:337
  67.0 10.4 %collective-permute-start.8 = (bf16[2,64,1024]{2,1,0:T(8,128)(2,1)S(1)}, bf16[2,64,1024]{2,1,0:T(8,128)(2,1)S(1)}, u32[]{:S(2)}, u32[]{:S(2)}) collective-permute-start(bf16[2,64,1024]{2,1,0:T(8,128)(2,1)S(1)} %pad_maximum_fusion.3), channel_id=1, source_target_pairs={{0,128},{128,0},{1,129},{129,1},{2,130},{130,2},{3,131},{131,3},{4... | collective-permute-start | bytes 786440 | tf_op jit(solution)/shard_map/ppermute | solution.py:337
  78.4 16.3 %all-to-all-start.1 = ((bf16[8,64,512]{2,1,0:T(8,128)(2,1)}), bf16[8,64,512]{2,1,0:T(8,128)(2,1)S(1)}, u32[]{:S(2)}, u32[]{:S(2)}) async-start(bf16[8,64,512]{2,1,0:T(8,128)(2,1)} %bitcast.8), calls=%async_computation.1 | async-start | bytes 1048576 | tf_op jit(solution)/shard_map/all_to_all | solution.py:390
